TPU v7x, 256 devices: a whole 4x4x8 slice. The times are simulated.
256 devices in a mesh: rep: 32 (over x, z), shard: 8 (over y, core).
Axes of the slice: x: 4, y: 4, z: 8, core: 2. Of those that a mesh axis runs over, the one named last changes fastest.
Arguments:
- grads: bfloat16 [32, 8, 1024, 3968], P('rep', 'shard'), may hold values from -6 to 6
- error: float32 [32, 1024, 3968], P('rep', 'shard'), may hold values from -6 to 6
- q_factor: float32 [32, 3968], replicated, may hold values from -0.09375 to 0.09375
Outputs:
- approx: float32 [1024, 3968], P('shard')
- new_error: float32 [32, 1024, 3968], P('rep', 'shard')
- q_next: float32 [32, 3968], replicated
All inputs are finite; a program needn't handle non-finite values.
Results may differ from a plain program's by a relative error of at most 0.0003.
Values sent between devices are 32-bit elements; how exact they have to be, the bound alone decides.
A program may use at most 128 MiB of HBM per device.

v0:
```python
import jax
import jax.numpy as jnp
from jax import lax
from jax.sharding import PartitionSpec as P


def body(grads, error, q_factor):
    local_grad = grads[0, 0].astype(jnp.float32)
    own_error = error[0]
    reduced = lax.psum_scatter(local_grad, "shard", scatter_dimension=0, tiled=True)
    merged = reduced + own_error
    factor_term = jnp.dot(
        merged, q_factor.T, precision=lax.Precision.HIGHEST, preferred_element_type=jnp.float32
    )
    own_factor = lax.psum(factor_term, "rep")
    gram_part = jnp.dot(
        own_factor.T,
        own_factor,
        precision=lax.Precision.HIGHEST,
        preferred_element_type=jnp.float32,
    )
    gram_matrix = lax.psum(gram_part, "shard")
    lower_factor = jnp.linalg.cholesky(gram_matrix)
    basis_rows = jax.scipy.linalg.solve_triangular(lower_factor, own_factor.T, lower=True)
    q_term = jnp.dot(
        basis_rows, merged, precision=lax.Precision.HIGHEST, preferred_element_type=jnp.float32
    )
    q_total_sum = lax.psum(q_term, ("rep", "shard"))
    q_next = q_total_sum / lax.axis_size("rep")
    approx = jnp.dot(
        basis_rows.T, q_next, precision=lax.Precision.HIGHEST, preferred_element_type=jnp.float32
    )
    new_error = merged - approx
    return (approx, new_error[None], q_next)


def solution(mesh):
    in_specs = (P("rep", "shard", None, None), P("rep", "shard", None), P())
    out_specs = (P("shard", None), P("rep", "shard", None), P())
    return jax.shard_map(body, mesh=mesh, in_specs=in_specs, out_specs=out_specs, check_vma=False)
```

profile of v0, /device:TPU:1, one launch (start us, length us, event | category | flops | bytes accessed | tf_op | source)
XLA Modules:
  0.0 547.6 jit_solution(1899689412729851559)
XLA Ops:
  7.2 0.0 copy-start
  7.2 0.0 reduce-scatter.2.cloned.1.call-start
  7.2 10.0 %bitcast_convert_fusion = f32[1024,3968]{1,0:T(8,128)} fusion(bf16[1,1,1024,3968]{3,2,1,0:T(8,128)(2,1)} %param.3), kind=kLoop, calls=%fused_computation | loop fusion | flops 4063232 | bytes 24379392 | tf_op jit(solution)/shard_map/convert_element_type | solution.py:8
  17.2 0.0 copy-start.1
  17.2 0.0 reduce-scatter.2.cloned.1.call-update
  17.3 0.0 all-reduce.2.cloned.1.call-start
  17.3 95.2 %reduce-scatter.2.cloned.1.call-done = f32[128,3968]{1,0:T(8,128)} async-done(((f32[1024,3968]{1,0:T(8,128)}), f32[128,3968]{1,0:T(8,128)}) %reduce-scatter.2.cloned.1.call-update) | async-done | bytes 2031632 | tf_op jit(solution)/shard_map/reduce_scatter | solution.py:10
  112.5 0.0 copy-done
  112.5 0.0 copy-done.1
  112.5 3.6 fusion.5
  116.1 115.4 %psum.21 = f32[128,32]{0,1:T(8,128)S(1)} all-reduce(f32[128,32]{0,1:T(8,128)S(1)} %fusion.5), channel_id=1, replica_groups=mesh['rep'=32,'shard'=8] {'rep'}, use_global_device_ids=true, to_apply=%region_1.0 | all-reduce | flops 4096 | bytes 32768 | tf_op jit(solution)/shard_map/psum | solution.py:15
  231.4 0.1 fusion.6
  231.6 49.0 %psum.22 = f32[32,32]{0,1:T(8,128)S(1)} all-reduce(f32[32,32]{0,1:T(8,128)S(1)} %fusion.6), channel_id=1, replica_groups=mesh['rep'=32,'shard'=8] {'shard'}, use_global_device_ids=true, to_apply=%region_2.0 | all-reduce | flops 1024 | bytes 8192 | tf_op jit(solution)/shard_map/psum | solution.py:22
  280.6 0.1 copy.7
  280.6 2.9 cholesky.16
  283.6 0.6 compare_reduce_fusion
  284.2 0.7 fusion
  284.9 2.4 custom-call.7
  287.3 0.2 fusion.1
  287.6 3.6 fusion.4
  291.2 0.0 all-reduce.2.cloned.1.call-update
  291.2 244.6 %all-reduce.2.cloned.1.call-done = f32[32,3968]{1,0:T(8,128)} async-done(((f32[32,3968]{1,0:T(8,128)}), f32[32,3968]{1,0:T(8,128)}) %all-reduce.2.cloned.1.call-update) | async-done | bytes 507920 | tf_op jit(solution)/shard_map/psum | solution.py:28
  535.8 0.0 copy-start.2
  535.8 1.2 broadcast_multiply_fusion
  537.0 0.0 copy-start.4
  537.0 1.8 fusion.7
  538.8 0.0 copy-done.2
  538.8 0.0 copy-start.3
  538.9 1.8 subtract_bitcast_fusion
  540.6 0.0 copy-done.4
  540.6 0.2 copy-done.3
  (2 shorter events, 0.0 us)
Async XLA Ops:
  7.2 105.3 %copy-start = (f32[32,3968]{1,0:T(8,128)S(1)}, f32[32,3968]{1,0:T(8,128)}, u32[]{:S(2)}) copy-start(f32[32,3968]{1,0:T(8,128)} %param.5) | copy-start | bytes 1523716
  7.2 105.3 %reduce-scatter.2.cloned.1.call-start = ((), (), s32[]{:S(2)}) async-start(), calls=%async_computation.1 | async-start | bytes 18284544 | tf_op jit(solution)/shard_map/reduce_scatter | solution.py:10
  17.2 95.3 %copy-start.1 = (f32[1,128,3968]{2,1,0:T(8,128)S(1)}, f32[1,128,3968]{2,1,0:T(8,128)}, u32[]{:S(2)}) copy-start(f32[1,128,3968]{2,1,0:T(8,128)} %param.4) | copy-start | bytes 6094852
  17.3 518.5 %all-reduce.2.cloned.1.call-start = ((), (), s32[]{:S(2)}) async-start(), calls=%async_computation.2 | async-start | bytes 1015808 | tf_op jit(solution)/shard_map/psum | solution.py:28
  535.8 3.0 copy-start.2
  537.0 3.6 copy-start.4
  538.8 2.0 copy-start.3
Sparse Core Ops, SparseCore 0:
  17.4 95.0 reduce-scatter.1
  291.3 244.4 all-reduce.1
where the time goes:
time: 548 us
  waiting for transfers between devices  340 us (62%)
  blocking collectives  164 us (30%)
  other arithmetic  19.7 us (4%)
  between operations  14.1 us (3%)
  matrix products  9.34 us (2%)
    psum x1, waiting for transfers between devices, body(): q_total_sum = lax.psum(q_term, ('rep', 'shard'))  245 us
    psum x1, blocking collectives, body(): own_factor = lax.psum(factor_term, 'rep')  115 us
    reduce_scatter x1, waiting for transfers between devices, body(): lax.psum_scatter(local_grad, 'shard', scatter_dimension=0, tiled=True)  95.2 us
    psum x1, blocking collectives, body(): gram_matrix = lax.psum(gram_part, 'shard')  49 us
  transfers between devices with their start and end apart: 2, of which 2 were waited for; matrix products, arithmetic and copies ran while one was open for 0% of the time, Pallas kernels for 0%

commit v1 on v0

v1 whole, which is shorter than its diff:
```python
import functools

import jax
import jax.numpy as jnp
from jax import lax
from jax.experimental import pallas as pl
from jax.experimental.pallas import tpu as pltpu
from jax.sharding import PartitionSpec as P

MESH = pl.DeviceIdType.MESH
F32 = jnp.float32
BF16 = jnp.bfloat16
HIGHEST = lax.Precision.HIGHEST
ROWS, COLS, RANK = 1024, 3968, 32
NX, NY, NZ = 4, 4, 8
OWN = 128
HALF = OWN // 2
CHUNK = 16
N_CHUNK = HALF // CHUNK
WIDE = 4096
NT = (((1,), (1,)), ((), ()))
NN = (((1,), (0,)), ((), ()))


def split3(value):
    high = value.astype(BF16)
    rest = value - high.astype(F32)
    middle = rest.astype(BF16)
    low = (rest - middle.astype(F32)).astype(BF16)
    return jnp.concatenate([high, middle, low], axis=0)


def fold3(value):
    return value[:RANK] + value[RANK : 2 * RANK] + value[2 * RANK :]


def inverse_lower(gram):
    row = lax.broadcasted_iota(jnp.int32, (RANK, 2 * RANK), 0)
    col = lax.broadcasted_iota(jnp.int32, (RANK, 2 * RANK), 1)
    work = jnp.concatenate([gram, jnp.zeros((RANK, RANK), F32)], axis=1)
    work = jnp.where(col == row + RANK, 1.0, work)
    scale = jnp.zeros((RANK, 1), F32)
    row1 = lax.broadcasted_iota(jnp.int32, (RANK, 1), 0)
    for j in range(RANK):
        pivot_row = work[j : j + 1, :]
        pivot = work[j : j + 1, j : j + 1]
        factor = jnp.where(row1 > j, work[:, j : j + 1] / pivot, 0.0)
        scale = jnp.where(row1 == j, 1.0 / jnp.sqrt(pivot), scale)
        work = work - factor * pivot_row
    return work[:, RANK:] * scale


def main_kernel(
    g_hbm, e_hbm, q_hbm,
    merged_hbm, usum_hbm, linv_ref, basis_ref,
    g, err, q, qs, psend, precv, far, near, merged, fs, linv,
    bufs_f, bufs_u,
    load_sem, out_sem, p_ss, p_rs, f_ss, f_rs, n_ss, n_rs, ar_f, ar_u,
):
    rep, shard = lax.axis_index("rep"), lax.axis_index("shard")
    x, z = rep // NZ, rep % NZ
    y, c = shard // 2, shard % 2

    def dev(dx, dy, dz, dc):
        return (
            ((x + dx) % NX) * NZ + (z + dz) % NZ,
            ((y + dy) % NY) * 2 + (c + dc) % 2,
        )

    partner = dev(0, 0, 0, 1)
    up, down = dev(0, 1, 0, 0), dev(0, NY - 1, 0, 0)
    x_peers = [dev(j, 0, 0, 0) for j in range(1, NX)]
    z_peers = [dev(0, 0, j, 0) for j in range(1, NZ)]
    y_peers = [dev(2, j, 0, 0) for j in range(1, NY)]
    peers = [partner, up, down, *x_peers, *z_peers, *y_peers]
    sent = []

    def send(src, dst, ss, rs, to):
        copy = pltpu.make_async_remote_copy(
            src_ref=src, dst_ref=dst, send_sem=ss, recv_sem=rs,
            device_id=to, device_id_type=MESH,
        )
        copy.start()
        sent.append(copy)
        return copy

    def first_row(k, t):
        return pl.multiple_of(OWN * (2 * ((y + k) % NY) + (c + t) % 2), OWN)

    def at(k, t):
        return OWN * (2 * k + t)

    q_load = pltpu.make_async_copy(q_hbm, q, load_sem.at[8])
    e_load = pltpu.make_async_copy(e_hbm.at[0], err, load_sem.at[9])
    loads = {}
    for k in (2, 1, 3, 0):
        for t in (1, 0):
            loads[k, t] = pltpu.make_async_copy(
                g_hbm.at[0, 0, pl.ds(first_row(k, t), OWN)],
                g.at[pl.ds(at(k, t), OWN)],
                load_sem.at[2 * k + t],
            )
            loads[k, t].start()
        if k == 2:
            q_load.start()
    e_load.start()

    barrier = pltpu.get_barrier_semaphore()
    for peer in peers:
        pl.semaphore_signal(barrier, 1, device_id=peer, device_id_type=MESH)

    def widen(k, start, rows):
        def step(i, carry):
            at_row = pl.multiple_of(start + i * CHUNK, CHUNK)
            psend[k, pl.ds(at_row, CHUNK), :] = g[
                pl.ds(at(k, 1) + at_row, CHUNK), :
            ].astype(F32)
            return carry

        lax.fori_loop(0, rows // CHUNK, step, 0)

    def to_partner(k, start, rows, i):
        window = (k, pl.ds(start, rows))
        return send(psend.at[window], precv.at[window], p_ss.at[i], p_rs.at[i], partner)

    def add_own(k, start, rows):
        def step(i, carry):
            at_row = pl.multiple_of(start + i * CHUNK, CHUNK)
            precv[k, pl.ds(at_row, CHUNK), :] += g[
                pl.ds(at(k, 0) + at_row, CHUNK), :
            ].astype(F32)
            return carry

        lax.fori_loop(0, rows // CHUNK, step, 0)

    loads[2, 1].wait()
    widen(2, 0, OWN)
    q_load.wait()
    qs[...] = split3(q[...])
    loads[2, 0].wait()
    pl.semaphore_wait(barrier, len(peers))

    order = [(d, i) for i in range(N_CHUNK) for d in (0, 1)]
    copies = {}
    for d, i in order:
        copies[d, i] = to_partner(2, d * HALF + i * CHUNK, CHUNK, d * N_CHUNK + i)
    far_copies = {}
    for d, i in order:
        start = d * HALF + i * CHUNK
        copies[d, i].wait_recv()
        add_own(2, start, CHUNK)
        far_copies[d, i] = send(
            precv.at[2, pl.ds(start, CHUNK)],
            far.at[d, pl.ds(i * CHUNK, CHUNK)],
            f_ss.at[d, i], f_rs.at[d, i], (up, down)[d],
        )

    loads[1, 1].wait()
    loads[1, 0].wait()
    widen(1, HALF, HALF)
    early_up = to_partner(1, HALF, HALF, 8)
    loads[3, 1].wait()
    loads[3, 0].wait()
    widen(3, 0, HALF)
    early_down = to_partner(3, 0, HALF, 9)
    later = {}
    near_copies = {}

    def send_near(d, start, i):
        near_copies[d, i] = send(
            precv.at[(1, 3)[d], pl.ds(start, HALF)],
            near.at[d, pl.ds(start, HALF)],
            n_ss.at[d, i], n_rs.at[d, i], (up, down)[d],
        )

    def near_early():
        early_up.wait_recv()
        add_own(1, HALF, HALF)
        send_near(0, HALF, 0)
        early_down.wait_recv()
        add_own(3, 0, HALF)
        send_near(1, 0, 0)

    def widen_rest():
        widen(1, 0, HALF)
        later[1] = to_partner(1, 0, HALF, 10)
        widen(3, HALF, HALF)
        later[3] = to_partner(3, HALF, HALF, 11)
        widen(0, 0, OWN)
        later[0] = to_partner(0, 0, OWN, 12)

    def near_late():
        for d, k, start in ((0, 1, 0), (1, 3, HALF)):
            later[k].wait_recv()
            for i in range(N_CHUNK):
                far_copies[d, i].wait_recv()

            def step(i, carry, d=d, k=k, start=start):
                at_row = pl.multiple_of(i * CHUNK, CHUNK)
                precv[k, pl.ds(start + at_row, CHUNK), :] = (
                    precv[k, pl.ds(start + at_row, CHUNK), :]
                    + g[pl.ds(at(k, 0) + start + at_row, CHUNK), :].astype(F32)
                    + far[d, pl.ds(at_row, CHUNK), :]
                )
                return carry

            lax.fori_loop(0, N_CHUNK, step, 0)
            send_near(d, start, 1)

    def merge_own():
        later[0].wait_recv()

        def step(i, carry):
            here = pl.ds(pl.multiple_of(i * CHUNK, CHUNK), CHUNK)
            merged[here, :] = (
                precv[0, here, :] + g[here, :].astype(F32) + err[here, :]
            )
            return carry

        lax.fori_loop(0, OWN // CHUNK, step, 0)

    def merge_near(d, i):
        start = ((HALF, 0), (0, HALF))[d][i]
        near_copies[d, i].wait_recv()

        def step(j, carry):
            here = pl.ds(pl.multiple_of(start + j * CHUNK, CHUNK), CHUNK)
            merged[here, :] += near[d, here, :]
            return carry

        lax.fori_loop(0, N_CHUNK, step, 0)

    def all_reduce(width, bufs, sems, beside):
        part, core_in, z_in, x_all, y_all, full = bufs
        ss, rs = sems
        piece = width // NZ
        mine = pl.multiple_of(16 * c, 16)
        theirs = pl.multiple_of(16 * (1 - c), 16)
        at_z = pl.multiple_of(piece * z, 128)

        copy = send(part.at[pl.ds(theirs, 16)], core_in, ss.at[0], rs.at[0], partner)
        beside("core")
        copy.wait_recv()
        core_in[...] += part[pl.ds(mine, 16), :]

        copies = []
        for j, peer in enumerate(z_peers):
            there = pl.multiple_of(piece * ((z + j + 1) % NZ), 128)
            copies.append(
                send(core_in.at[:, pl.ds(there, piece)], z_in.at[j], ss.at[1 + j], rs.at[1 + j], peer)
            )
        beside("z")
        total = core_in[:, pl.ds(at_z, piece)]
        for j, copy in enumerate(copies):
            copy.wait_recv()
            total = total + z_in[j]
        x_all[x] = total

        copies = [
            send(x_all.at[x], x_all.at[x], ss.at[8 + j], rs.at[8 + j], peer)
            for j, peer in enumerate(x_peers)
        ]
        beside("x")
        for copy in copies:
            copy.wait_recv()
        y_all[y] = (x_all[0] + x_all[1]) + (x_all[2] + x_all[3])

        copies = [
            send(y_all.at[y], y_all.at[y], ss.at[11 + j], rs.at[11 + j], peer)
            for j, peer in enumerate(y_peers)
        ]
        beside("y")
        for copy in copies:
            copy.wait_recv()
        window = (pl.ds(mine, 16), pl.ds(at_z, piece))
        full[window] = (y_all[0] + y_all[1]) + (y_all[2] + y_all[3])

        copies = [
            send(full.at[window], full.at[window], ss.at[14 + j], rs.at[14 + j], peer)
            for j, peer in enumerate(z_peers)
        ]
        beside("z2")
        for copy in copies:
            copy.wait_recv()

        window = (pl.ds(mine, 16),)
        copy = send(full.at[window], full.at[window], ss.at[21], rs.at[21], partner)
        beside("core2")
        copy.wait_recv()

    loads[0, 1].wait()
    loads[0, 0].wait()
    e_load.wait()
    part_f = bufs_f[0]
    for k in range(NY):
        terms = fold3(
            lax.dot_general(qs[...], g[pl.ds(at(k, 0), 2 * OWN), :], NT, preferred_element_type=F32)
        )
        for t in (0, 1):
            term = terms[:, OWN * t : OWN * (t + 1)]
            if (k, t) == (0, 0):
                term = term + lax.dot_general(
                    q[...], err[...], NT, precision=HIGHEST, preferred_element_type=F32
                )
            part_f[:, pl.ds(first_row(k, t), OWN)] = term

    def beside_f(phase):
        if phase == "core":
            near_early()
        elif phase == "z":
            widen_rest()
        elif phase == "z2":
            near_late()

    all_reduce(ROWS, bufs_f, ar_f, beside_f)
    factor = bufs_f[5]

    for k in range(NY):
        for t in (0, 1):
            fs[:, pl.ds(at(k, t), OWN)] = split3(factor[:, pl.ds(first_row(k, t), OWN)])
    own_factor = factor[:, pl.ds(first_row(0, 0), OWN)]
    part_u = bufs_u[0]
    for start in range(0, COLS, 1024):
        cols = pl.ds(start, min(1024, COLS - start))
        part_u[:, cols] = fold3(
            lax.dot_general(fs[...], g[:, cols], NN, preferred_element_type=F32)
        ) + lax.dot_general(own_factor, err[:, cols], NN, precision=HIGHEST, preferred_element_type=F32)
    part_u[:, pl.ds(COLS, WIDE - COLS)] = jnp.zeros((RANK, WIDE - COLS), F32)

    def beside_u(phase):
        if phase == "z":
            merge_own()
            whole = factor[...]
            gram = lax.dot_general(whole, whole, NT, precision=HIGHEST, preferred_element_type=F32)
            linv[...] = inverse_lower(gram)
        elif phase == "x":
            linv_ref[...] = linv[...]
            basis_ref[...] = lax.dot_general(
                linv[...], own_factor, NN, precision=HIGHEST, preferred_element_type=F32
            )
        elif phase == "z2":
            merge_near(0, 0)
            merge_near(1, 0)

    all_reduce(WIDE, bufs_u, ar_u, beside_u)
    usum_out = pltpu.make_async_copy(
        bufs_u[5].at[:, pl.ds(0, COLS)], usum_hbm, out_sem.at[0]
    )
    usum_out.start()
    outs = [usum_out]
    for d, start in ((0, 0), (1, HALF)):
        merge_near(d, 1)
        copy = pltpu.make_async_copy(
            merged.at[pl.ds(start, HALF)], merged_hbm.at[pl.ds(start, HALF)], out_sem.at[1 + d]
        )
        copy.start()
        outs.append(copy)
    for copy in sent:
        copy.wait_send()
    for copy in outs:
        copy.wait()


def reduce_buffers(width):
    piece = width // NZ
    return (
        pltpu.VMEM((RANK, width), F32),
        pltpu.VMEM((16, width), F32),
        pltpu.VMEM((NZ - 1, 16, piece), F32),
        pltpu.VMEM((NX, 16, piece), F32),
        pltpu.VMEM((NY, 16, piece), F32),
        pltpu.VMEM((RANK, width), F32),
    )


def final_kernel(n_rep, merged, usum, linv, basis, approx, new_error, q_next):
    @pl.when(pl.program_id(0) == 0)
    def _():
        q_next[...] = lax.dot_general(
            linv[...], usum[...], NN, precision=HIGHEST, preferred_element_type=F32
        ) * (1.0 / n_rep)

    value = lax.dot_general(
        basis[...], q_next[...], NN, precision=HIGHEST, preferred_element_type=F32
    )
    approx[...] = value
    new_error[0] = merged[...] - value


def body(grads, error, q_factor):
    any_space = pl.BlockSpec(memory_space=pl.ANY)
    vmem = pl.BlockSpec(memory_space=pltpu.VMEM)
    dma = pltpu.SemaphoreType.DMA
    merged, usum, linv, basis_t = pl.pallas_call(
        main_kernel,
        out_shape=(
            jax.ShapeDtypeStruct((OWN, COLS), F32),
            jax.ShapeDtypeStruct((RANK, COLS), F32),
            jax.ShapeDtypeStruct((RANK, RANK), F32),
            jax.ShapeDtypeStruct((RANK, OWN), F32),
        ),
        in_specs=[any_space] * 3,
        out_specs=(any_space, any_space, vmem, vmem),
        scratch_shapes=[
            pltpu.VMEM((ROWS, COLS), BF16),
            pltpu.VMEM((OWN, COLS), F32),
            pltpu.VMEM((RANK, COLS), F32),
            pltpu.VMEM((3 * RANK, COLS), BF16),
            pltpu.VMEM((NY, OWN, COLS), F32),
            pltpu.VMEM((NY, OWN, COLS), F32),
            pltpu.VMEM((2, HALF, COLS), F32),
            pltpu.VMEM((2, OWN, COLS), F32),
            pltpu.VMEM((OWN, COLS), F32),
            pltpu.VMEM((3 * RANK, ROWS), BF16),
            pltpu.VMEM((RANK, RANK), F32),
            reduce_buffers(ROWS),
            reduce_buffers(WIDE),
            dma((10,)),
            dma((3,)),
            dma((13,)),
            dma((13,)),
            dma((2, N_CHUNK)),
            dma((2, N_CHUNK)),
            dma((2, 2)),
            dma((2, 2)),
            (dma((22,)), dma((22,))),
            (dma((22,)), dma((22,))),
        ],
        compiler_params=pltpu.CompilerParams(
            collective_id=0, has_side_effects=True, vmem_limit_bytes=56 << 20
        ),
        cost_estimate=pl.CostEstimate(
            flops=1 << 31, bytes_accessed=14 << 20, transcendentals=0
        ),
    )(grads, error, q_factor)
    step = 32
    rows = pl.BlockSpec((step, COLS), lambda i: (i, 0))
    whole = pl.BlockSpec((RANK, COLS), lambda i: (0, 0))
    return pl.pallas_call(
        functools.partial(final_kernel, lax.axis_size("rep")),
        grid=(OWN // step,),
        out_shape=(
            jax.ShapeDtypeStruct((OWN, COLS), F32),
            jax.ShapeDtypeStruct((1, OWN, COLS), F32),
            jax.ShapeDtypeStruct((RANK, COLS), F32),
        ),
        in_specs=[
            rows,
            whole,
            pl.BlockSpec((RANK, RANK), lambda i: (0, 0)),
            pl.BlockSpec((step, RANK), lambda i: (i, 0)),
        ],
        out_specs=(rows, pl.BlockSpec((1, step, COLS), lambda i: (0, i, 0)), whole),
        compiler_params=pltpu.CompilerParams(vmem_limit_bytes=32 << 20),
    )(merged, usum, linv, basis_t.T)


def solution(mesh):
    in_specs = (P("rep", "shard", None, None), P("rep", "shard", None), P())
    out_specs = (P("shard", None), P("rep", "shard", None), P())
    return jax.shard_map(body, mesh=mesh, in_specs=in_specs, out_specs=out_specs, check_vma=False)
```

time: 548 us -> 93.1 us (0.17)
  waiting for transfers between devices: 340 us -> 0 us
  blocking collectives: 164 us -> 0 us
  Pallas kernels: 0 us -> 88.1 us
  other arithmetic: 19.7 us -> 0 us
  between operations: 14.1 us -> 0.65 us
  matrix products: 9.34 us -> 0 us
    psum x1 -> x0, waiting for transfers between devices: 245 us -> none  [body(): q_total_sum = lax.psum(q_term, ('rep', 'shard'))]
    psum x2 -> x0, blocking collectives: 164 us -> none  [the longest x1 115 us: body(): own_factor = lax.psum(factor_term, 'rep')]
    reduce_scatter x1 -> x0, waiting for transfers between devices: 95.2 us -> none  [body(): lax.psum_scatter(local_grad, 'shard', scatter_dimension=0, tiled=True)]
    pallas_call x0 -> x2, Pallas kernels: none -> 88.1 us  [the longest x1 83.9 us: body(): pl.pallas_call(main_kernel, out_shape=(jax.ShapeDtypeStruct((OWN, COLS),...]
    convert_element_type x1 -> x0, other arithmetic: 10 us -> none  [body(): local_grad = grads[0, 0].astype(jnp.float32)]
    dot_general x4 -> x0, matrix products: 9.11 us -> none  [the longest x1 3.61 us: body(): jnp.dot(basis_rows, merged, precision=lax.Precision.HIGHEST, preferred_el...]
    another operation x5 -> x0, other arithmetic: 6.68 us -> none  [the longest x3 3.59 us: body(): lower_factor = jnp.linalg.cholesky(gram_matrix)]
  transfers between devices with their start and end apart: 2 -> 0, of which waited for: 2 -> 0; matrix products, arithmetic and copies ran while one was open for 0% -> 0% of each run, Pallas kernels for 0% -> 0%
where the time goes in v1:
time: 93.1 us; the launch traced here: 92.8 us
  Pallas kernels  88.1 us (95%)
  local copies, waits for them, and re-layouts  4.13 us (4%)
    pallas_call x1, Pallas kernels, body(): pl.pallas_call(main_kernel, out_shape=(jax.ShapeDtypeStruct((OWN, COLS),...  83.9 us
    pallas_call x1, Pallas kernels, body(): pl.pallas_call(functools.partial(final_kernel, lax.axis_size('rep')), gri...  4.13 us
    unnamed x6, local copies, waits for them, and re-layouts  3.32 us

profile of v1, /device:TPU:1, one launch (start us, length us, event | category | flops | bytes accessed | tf_op | source)
XLA Modules:
  0.0 92.8 jit_solution(13884734531891276665)
XLA Ops:
  0.6 83.9 %shard_map.58 = (f32[128,3968]{1,0:T(8,128)}, f32[32,3968]{1,0:T(8,128)}, f32[32,32]{1,0:T(8,128)}, f32[32,128]{1,0:T(8,128)}) custom-call(bf16[1,1,1024,3968]{3,2,1,0:T(8,128)(2,1)} %g_hbm.1, f32[1,128,3968]{2,1,0:T(8,128)} %e_hbm.1, f32[32,3968]{1,0:T(8,128)} %q_hbm.1), custom_call_target="tpu_custom_call" | custom-call | flops 2147483648 | bytes 14680064 | tf_op jit(solution)/shard_map/pallas_call | solution.py:394
  84.6 0.8 copy.6
  85.4 0.0 copy-start
  85.4 1.6 %copy-done = f32[128,3968]{1,0:T(8,128)S(1)} copy-done((f32[128,3968]{1,0:T(8,128)S(1)}, f32[128,3968]{1,0:T(8,128)}, u32[]{:S(2)}) %copy-start) | copy-done | bytes 2031640
  87.0 0.0 copy-start.1
  87.0 1.0 %copy-done.1 = f32[32,3968]{1,0:T(8,128)S(1)} copy-done((f32[32,3968]{1,0:T(8,128)S(1)}, f32[32,3968]{1,0:T(8,128)}, u32[]{:S(2)}) %copy-start.1) | copy-done | bytes 507928
  88.0 0.0 copy-start.2
  88.0 0.7 copy-done.2
  88.7 4.1 %shard_map.59 = (f32[128,3968]{1,0:T(8,128)}, f32[1,128,3968]{2,1,0:T(8,128)}, f32[32,3968]{1,0:T(8,128)}) custom-call(f32[128,3968]{1,0:T(8,128)S(1)} %copy-done, f32[32,3968]{1,0:T(8,128)S(1)} %copy-done.1, f32[32,32]{1,0:T(8,128)S(1)} %copy-done.2, f32[128,32]{1,0:T(8,128)S(1)} %bitcast.1), custom_call_target="tpu_custom_call" | custom-call | tf_op jit(solution)/shard_map/pallas_call | solution.py:439
Async XLA Ops:
  85.4 1.6 %copy-start = (f32[128,3968]{1,0:T(8,128)S(1)}, f32[128,3968]{1,0:T(8,128)}, u32[]{:S(2)}) copy-start(f32[128,3968]{1,0:T(8,128)} %get-tuple-element.7.merged) | copy-start | bytes 6094852
  87.0 1.0 %copy-start.1 = (f32[32,3968]{1,0:T(8,128)S(1)}, f32[32,3968]{1,0:T(8,128)}, u32[]{:S(2)}) copy-start(f32[32,3968]{1,0:T(8,128)} %get-tuple-element.8.usum) | copy-start | bytes 1523716
  88.0 0.7 copy-start.2

commit v2 on v1

--- a/solution.py
+++ b/solution.py
@@ -17,9 +17,11 @@
 HALF = OWN // 2
 CHUNK = 16
 N_CHUNK = HALF // CHUNK
+N_PART = 4
 WIDE = 4096
 NT = (((1,), (1,)), ((), ()))
 NN = (((1,), (0,)), ((), ()))
+TN = (((0,), (0,)), ((), ()))
 
 
 def split3(value):
@@ -52,10 +54,10 @@
 
 def main_kernel(
     g_hbm, e_hbm, q_hbm,
-    merged_hbm, usum_hbm, linv_ref, basis_ref,
-    g, err, q, qs, psend, precv, far, near, merged, fs, linv,
+    approx, new_error, q_next,
+    g, err, q, qs, psend, precv, far, near, fs, linv, basis,
     bufs_f, bufs_u,
-    load_sem, out_sem, p_ss, p_rs, f_ss, f_rs, n_ss, n_rs, ar_f, ar_u,
+    load_sem, p_ss, p_rs, f_ss, f_rs, n_ss, n_rs, ar_f, ar_u, reply,
 ):
     rep, shard = lax.axis_index("rep"), lax.axis_index("shard")
     x, z = rep // NZ, rep % NZ
@@ -72,8 +74,19 @@
     x_peers = [dev(j, 0, 0, 0) for j in range(1, NX)]
     z_peers = [dev(0, 0, j, 0) for j in range(1, NZ)]
     y_peers = [dev(2, j, 0, 0) for j in range(1, NY)]
-    peers = [partner, up, down, *x_peers, *z_peers, *y_peers]
     sent = []
+    barrier = pltpu.get_barrier_semaphore()
+
+    def signal(semaphore, peer):
+        pl.semaphore_signal(semaphore, 1, device_id=peer, device_id_type=MESH)
+
+    def signal_far(semaphore, above):
+        for j, peer in enumerate(z_peers):
+            pl.when((z + j + 1 < NZ) == above)(functools.partial(signal, semaphore, peer))
+        for j, peer in enumerate(x_peers):
+            pl.when((x + j + 1 < NX) == above)(functools.partial(signal, semaphore, peer))
+        for peer in y_peers:
+            pl.when((x < 2) == above)(functools.partial(signal, semaphore, peer))
 
     def send(src, dst, ss, rs, to):
         copy = pltpu.make_async_remote_copy(
@@ -90,6 +103,8 @@
     def at(k, t):
         return OWN * (2 * k + t)
 
+    for peer in (partner, up, down):
+        signal(barrier, peer)
     q_load = pltpu.make_async_copy(q_hbm, q, load_sem.at[8])
     e_load = pltpu.make_async_copy(e_hbm.at[0], err, load_sem.at[9])
     loads = {}
@@ -102,12 +117,9 @@
             )
             loads[k, t].start()
         if k == 2:
+            signal_far(barrier, True)
             q_load.start()
     e_load.start()
-
-    barrier = pltpu.get_barrier_semaphore()
-    for peer in peers:
-        pl.semaphore_signal(barrier, 1, device_id=peer, device_id_type=MESH)
 
     def widen(k, start, rows):
         def step(i, carry):
@@ -135,15 +147,13 @@
 
     loads[2, 1].wait()
     widen(2, 0, OWN)
-    q_load.wait()
-    qs[...] = split3(q[...])
-    loads[2, 0].wait()
-    pl.semaphore_wait(barrier, len(peers))
+    pl.semaphore_wait(barrier, 3 + z + x + 3 * (x // 2))
 
     order = [(d, i) for i in range(N_CHUNK) for d in (0, 1)]
     copies = {}
     for d, i in order:
         copies[d, i] = to_partner(2, d * HALF + i * CHUNK, CHUNK, d * N_CHUNK + i)
+    loads[2, 0].wait()
     far_copies = {}
     for d, i in order:
         start = d * HALF + i * CHUNK
@@ -154,6 +164,8 @@
             far.at[d, pl.ds(i * CHUNK, CHUNK)],
             f_ss.at[d, i], f_rs.at[d, i], (up, down)[d],
         )
+
+    signal_far(reply, False)
 
     loads[1, 1].wait()
     loads[1, 0].wait()
@@ -166,20 +178,20 @@
     later = {}
     near_copies = {}
 
-    def send_near(d, start, i):
+    def send_near(d, start, rows, i):
         near_copies[d, i] = send(
-            precv.at[(1, 3)[d], pl.ds(start, HALF)],
-            near.at[d, pl.ds(start, HALF)],
+            precv.at[(1, 3)[d], pl.ds(start, rows)],
+            near.at[d, pl.ds(start, rows)],
             n_ss.at[d, i], n_rs.at[d, i], (up, down)[d],
         )
 
     def near_early():
         early_up.wait_recv()
         add_own(1, HALF, HALF)
-        send_near(0, HALF, 0)
+        send_near(0, HALF, HALF, N_CHUNK)
         early_down.wait_recv()
         add_own(3, 0, HALF)
-        send_near(1, 0, 0)
+        send_near(1, 0, HALF, N_CHUNK)
 
     def widen_rest():
         widen(1, 0, HALF)
@@ -190,45 +202,41 @@
         later[0] = to_partner(0, 0, OWN, 12)
 
     def near_late():
-        for d, k, start in ((0, 1, 0), (1, 3, HALF)):
-            later[k].wait_recv()
-            for i in range(N_CHUNK):
+        later[1].wait_recv()
+        later[3].wait_recv()
+        for i in range(N_CHUNK):
+            for d, k, start in ((0, 1, 0), (1, 3, HALF)):
                 far_copies[d, i].wait_recv()
-
-            def step(i, carry, d=d, k=k, start=start):
-                at_row = pl.multiple_of(i * CHUNK, CHUNK)
-                precv[k, pl.ds(start + at_row, CHUNK), :] = (
-                    precv[k, pl.ds(start + at_row, CHUNK), :]
-                    + g[pl.ds(at(k, 0) + start + at_row, CHUNK), :].astype(F32)
-                    + far[d, pl.ds(at_row, CHUNK), :]
+                here = pl.ds(start + i * CHUNK, CHUNK)
+                precv[k, here, :] = (
+                    precv[k, here, :]
+                    + g[pl.ds(at(k, 0) + start + i * CHUNK, CHUNK), :].astype(F32)
+                    + far[d, pl.ds(i * CHUNK, CHUNK), :]
                 )
-                return carry
-
-            lax.fori_loop(0, N_CHUNK, step, 0)
-            send_near(d, start, 1)
+                send_near(d, start + i * CHUNK, CHUNK, i)
 
     def merge_own():
         later[0].wait_recv()
 
         def step(i, carry):
             here = pl.ds(pl.multiple_of(i * CHUNK, CHUNK), CHUNK)
-            merged[here, :] = (
+            new_error[here, :] = (
                 precv[0, here, :] + g[here, :].astype(F32) + err[here, :]
             )
             return carry
 
         lax.fori_loop(0, OWN // CHUNK, step, 0)
 
-    def merge_near(d, i):
-        start = ((HALF, 0), (0, HALF))[d][i]
-        near_copies[d, i].wait_recv()
-
-        def step(j, carry):
-            here = pl.ds(pl.multiple_of(start + j * CHUNK, CHUNK), CHUNK)
-            merged[here, :] += near[d, here, :]
-            return carry
-
-        lax.fori_loop(0, N_CHUNK, step, 0)
+    def merge_early():
+        for d, start in ((0, HALF), (1, 0)):
+            near_copies[d, N_CHUNK].wait_recv()
+
+            def step(j, carry, d=d, start=start):
+                here = pl.ds(pl.multiple_of(start + j * CHUNK, CHUNK), CHUNK)
+                new_error[here, :] += near[d, here, :]
+                return carry
+
+            lax.fori_loop(0, N_CHUNK, step, 0)
 
     def all_reduce(width, bufs, sems, beside):
         part, core_in, z_in, x_all, y_all, full = bufs
@@ -291,6 +299,8 @@
     loads[0, 1].wait()
     loads[0, 0].wait()
     e_load.wait()
+    q_load.wait()
+    qs[...] = split3(q[...])
     part_f = bufs_f[0]
     for k in range(NY):
         terms = fold3(
@@ -307,6 +317,11 @@
     def beside_f(phase):
         if phase == "core":
             near_early()
+            answers = (NZ - 1 - z) + (NX - 1 - x) + 3 * (1 - x // 2)
+
+            @pl.when(answers > 0)
+            def _():
+                pl.semaphore_wait(reply, answers)
         elif phase == "z":
             widen_rest()
         elif phase == "z2":
@@ -334,31 +349,31 @@
             gram = lax.dot_general(whole, whole, NT, precision=HIGHEST, preferred_element_type=F32)
             linv[...] = inverse_lower(gram)
         elif phase == "x":
-            linv_ref[...] = linv[...]
-            basis_ref[...] = lax.dot_general(
+            basis[...] = lax.dot_general(
                 linv[...], own_factor, NN, precision=HIGHEST, preferred_element_type=F32
             )
         elif phase == "z2":
-            merge_near(0, 0)
-            merge_near(1, 0)
+            merge_early()
 
     all_reduce(WIDE, bufs_u, ar_u, beside_u)
-    usum_out = pltpu.make_async_copy(
-        bufs_u[5].at[:, pl.ds(0, COLS)], usum_hbm, out_sem.at[0]
-    )
-    usum_out.start()
-    outs = [usum_out]
-    for d, start in ((0, 0), (1, HALF)):
-        merge_near(d, 1)
-        copy = pltpu.make_async_copy(
-            merged.at[pl.ds(start, HALF)], merged_hbm.at[pl.ds(start, HALF)], out_sem.at[1 + d]
-        )
-        copy.start()
-        outs.append(copy)
+    for start in range(0, COLS, 1024):
+        cols = pl.ds(start, min(1024, COLS - start))
+        right = lax.dot_general(
+            linv[...], bufs_u[5][:, cols], NN, precision=HIGHEST, preferred_element_type=F32
+        ) * (1.0 / (NX * NZ))
+        q_next[:, cols] = right
+        value = lax.dot_general(
+            basis[...], right, TN, precision=HIGHEST, preferred_element_type=F32
+        )
+        approx[:, cols] = value
+        new_error[:, cols] -= value
+    for i in range(N_CHUNK):
+        for d, start in ((0, 0), (1, HALF)):
+            near_copies[d, i].wait_recv()
+            here = pl.ds(start + i * CHUNK, CHUNK)
+            new_error[here, :] += near[d, here, :]
     for copy in sent:
         copy.wait_send()
-    for copy in outs:
-        copy.wait()
 
 
 def reduce_buffers(width):
@@ -373,34 +388,37 @@
     )
 
 
-def final_kernel(n_rep, merged, usum, linv, basis, approx, new_error, q_next):
-    @pl.when(pl.program_id(0) == 0)
-    def _():
-        q_next[...] = lax.dot_general(
-            linv[...], usum[...], NN, precision=HIGHEST, preferred_element_type=F32
-        ) * (1.0 / n_rep)
-
-    value = lax.dot_general(
-        basis[...], q_next[...], NN, precision=HIGHEST, preferred_element_type=F32
-    )
-    approx[...] = value
-    new_error[0] = merged[...] - value
+def out_kernel(approx, new_error, q_next, approx_out, new_error_out, q_out, sem):
+    copies = [pltpu.make_async_copy(q_next, q_out, sem.at[0])]
+    for i in range(N_PART):
+        rows = pl.ds(i * (OWN // N_PART), OWN // N_PART)
+        copies.append(
+            pltpu.make_async_copy(approx.at[rows], approx_out.at[rows], sem.at[1 + 2 * i])
+        )
+        copies.append(
+            pltpu.make_async_copy(
+                new_error.at[rows], new_error_out.at[0, rows], sem.at[2 + 2 * i]
+            )
+        )
+    for copy in copies:
+        copy.start()
+    for copy in copies:
+        copy.wait()
 
 
 def body(grads, error, q_factor):
     any_space = pl.BlockSpec(memory_space=pl.ANY)
     vmem = pl.BlockSpec(memory_space=pltpu.VMEM)
     dma = pltpu.SemaphoreType.DMA
-    merged, usum, linv, basis_t = pl.pallas_call(
+    results = pl.pallas_call(
         main_kernel,
         out_shape=(
-            jax.ShapeDtypeStruct((OWN, COLS), F32),
-            jax.ShapeDtypeStruct((RANK, COLS), F32),
-            jax.ShapeDtypeStruct((RANK, RANK), F32),
-            jax.ShapeDtypeStruct((RANK, OWN), F32),
+            pltpu.VMEM((OWN, COLS), F32),
+            pltpu.VMEM((OWN, COLS), F32),
+            pltpu.VMEM((RANK, COLS), F32),
         ),
         in_specs=[any_space] * 3,
-        out_specs=(any_space, any_space, vmem, vmem),
+        out_specs=(vmem,) * 3,
         scratch_shapes=[
             pltpu.VMEM((ROWS, COLS), BF16),
             pltpu.VMEM((OWN, COLS), F32),
@@ -410,49 +428,41 @@
             pltpu.VMEM((NY, OWN, COLS), F32),
             pltpu.VMEM((2, HALF, COLS), F32),
             pltpu.VMEM((2, OWN, COLS), F32),
-            pltpu.VMEM((OWN, COLS), F32),
             pltpu.VMEM((3 * RANK, ROWS), BF16),
             pltpu.VMEM((RANK, RANK), F32),
+            pltpu.VMEM((RANK, OWN), F32),
             reduce_buffers(ROWS),
             reduce_buffers(WIDE),
             dma((10,)),
-            dma((3,)),
             dma((13,)),
             dma((13,)),
             dma((2, N_CHUNK)),
             dma((2, N_CHUNK)),
-            dma((2, 2)),
-            dma((2, 2)),
+            dma((2, N_CHUNK + 1)),
+            dma((2, N_CHUNK + 1)),
             (dma((22,)), dma((22,))),
             (dma((22,)), dma((22,))),
+            pltpu.SemaphoreType.REGULAR,
         ],
         compiler_params=pltpu.CompilerParams(
-            collective_id=0, has_side_effects=True, vmem_limit_bytes=56 << 20
+            collective_id=0, has_side_effects=True, vmem_limit_bytes=48 << 20
         ),
         cost_estimate=pl.CostEstimate(
             flops=1 << 31, bytes_accessed=14 << 20, transcendentals=0
         ),
-    )(grads, error, q_factor)
-    step = 32
-    rows = pl.BlockSpec((step, COLS), lambda i: (i, 0))
-    whole = pl.BlockSpec((RANK, COLS), lambda i: (0, 0))
+    )(grads, error, pltpu.with_memory_space_constraint(q_factor, pltpu.HBM))
     return pl.pallas_call(
-        functools.partial(final_kernel, lax.axis_size("rep")),
-        grid=(OWN // step,),
+        out_kernel,
         out_shape=(
             jax.ShapeDtypeStruct((OWN, COLS), F32),
             jax.ShapeDtypeStruct((1, OWN, COLS), F32),
             jax.ShapeDtypeStruct((RANK, COLS), F32),
         ),
-        in_specs=[
-            rows,
-            whole,
-            pl.BlockSpec((RANK, RANK), lambda i: (0, 0)),
-            pl.BlockSpec((step, RANK), lambda i: (i, 0)),
-        ],
-        out_specs=(rows, pl.BlockSpec((1, step, COLS), lambda i: (0, i, 0)), whole),
-        compiler_params=pltpu.CompilerParams(vmem_limit_bytes=32 << 20),
-    )(merged, usum, linv, basis_t.T)
+        in_specs=[vmem] * 3,
+        out_specs=(any_space,) * 3,
+        scratch_shapes=[dma((1 + 2 * N_PART,))],
+        compiler_params=pltpu.CompilerParams(vmem_limit_bytes=16 << 20),
+    )(*results)
 
 
 def solution(mesh):

time: 93.1 us -> 79.5 us (0.85)
  Pallas kernels: 88.1 us -> 78.7 us
  local copies, waits for them, and re-layouts: 4.13 us -> 0 us
    pallas_call x2, Pallas kernels: 88.1 us -> 78.7 us  [the longest x1 76.5 us: body(): pl.pallas_call(main_kernel, out_shape=(pltpu.VMEM((OWN, COLS), F32), pltp...]
    unnamed x6 -> x0, local copies, waits for them, and re-layouts: 3.32 us -> none
where the time goes in v2:
time: 79.5 us; the launch traced here: 79.4 us
  Pallas kernels  78.7 us (99%)
    pallas_call x1, Pallas kernels, body(): pl.pallas_call(main_kernel, out_shape=(pltpu.VMEM((OWN, COLS), F32), pltp...  76.5 us
    pallas_call x1, Pallas kernels, body(): pl.pallas_call(out_kernel, out_shape=(jax.ShapeDtypeStruct((OWN, COLS), F...  2.2 us

profile of v2, /device:TPU:1, one launch (start us, length us, event | category | flops | bytes accessed | tf_op | source)
XLA Modules:
  0.0 79.4 jit_solution(15920747804118644907)
XLA Ops:
  0.6 76.5 %shard_map.58 = (f32[128,3968]{1,0:T(8,128)S(1)}, f32[128,3968]{1,0:T(8,128)S(1)}, f32[32,3968]{1,0:T(8,128)S(1)}) custom-call(bf16[1,1,1024,3968]{3,2,1,0:T(8,128)(2,1)} %g_hbm.1, f32[1,128,3968]{2,1,0:T(8,128)} %e_hbm.1, f32[32,3968]{1,0:T(8,128)} %q_hbm.1), custom_call_target="tpu_custom_call" | custom-call | flops 2147483648 | bytes 14680064 | tf_op jit(solution)/shard_map/pallas_call | solution.py:413
  77.2 2.2 %shard_map.59 = (f32[128,3968]{1,0:T(8,128)}, f32[1,128,3968]{2,1,0:T(8,128)}, f32[32,3968]{1,0:T(8,128)}) custom-call(f32[128,3968]{1,0:T(8,128)S(1)} %get-tuple-element.6.approx, f32[128,3968]{1,0:T(8,128)S(1)} %get-tuple-element.7.new_error, f32[32,3968]{1,0:T(8,128)S(1)} %get-tuple-element.8.q_next), custom_call_target="tpu_custom_call" | custom-call | tf_op jit(solution)/shard_map/pallas_call | solution.py:454

commit v3 on v2

--- a/solution.py
+++ b/solution.py
@@ -21,19 +21,32 @@
 WIDE = 4096
 NT = (((1,), (1,)), ((), ()))
 NN = (((1,), (0,)), ((), ()))
-TN = (((0,), (0,)), ((), ()))
-
-
-def split3(value):
+
+
+def split(value):
     high = value.astype(BF16)
     rest = value - high.astype(F32)
     middle = rest.astype(BF16)
     low = (rest - middle.astype(F32)).astype(BF16)
-    return jnp.concatenate([high, middle, low], axis=0)
+    return high, middle, low
+
+
+def split3(value):
+    return jnp.concatenate(split(value), axis=0)
+
+
+def left6(value):
+    high, middle, low = (term.astype(F32) for term in split(value))
+    return jnp.concatenate([high, high, middle, high, low, middle], axis=0).T.astype(BF16)
+
+
+def right6(value):
+    high, middle, low = split(value)
+    return jnp.concatenate([high, middle, high, low, high, middle], axis=0)
 
 
 def fold3(value):
-    return value[:RANK] + value[RANK : 2 * RANK] + value[2 * RANK :]
+    return value[:RANK] + value[RANK : 2 * RANK] + value[2 * RANK : 3 * RANK]
 
 
 def inverse_lower(gram):
@@ -55,9 +68,9 @@
 def main_kernel(
     g_hbm, e_hbm, q_hbm,
     approx, new_error, q_next,
-    g, err, q, qs, psend, precv, far, near, fs, linv, basis,
+    g, err, q, qs, psend, precv, far, near, fs, linv6, basis6,
     bufs_f, bufs_u,
-    load_sem, p_ss, p_rs, f_ss, f_rs, n_ss, n_rs, ar_f, ar_u, reply,
+    load_sem, far_sem, p_ss, p_rs, f_ss, f_rs, n_ss, n_rs, ar_f, ar_u, reply, ring,
 ):
     rep, shard = lax.axis_index("rep"), lax.axis_index("shard")
     x, z = rep // NZ, rep % NZ
@@ -80,13 +93,14 @@
     def signal(semaphore, peer):
         pl.semaphore_signal(semaphore, 1, device_id=peer, device_id_type=MESH)
 
+    def place(at_x):
+        return at_x + (at_x == 2) - (at_x == 3)
+
     def signal_far(semaphore, above):
         for j, peer in enumerate(z_peers):
             pl.when((z + j + 1 < NZ) == above)(functools.partial(signal, semaphore, peer))
         for j, peer in enumerate(x_peers):
-            pl.when((x + j + 1 < NX) == above)(functools.partial(signal, semaphore, peer))
-        for peer in y_peers:
-            pl.when((x < 2) == above)(functools.partial(signal, semaphore, peer))
+            pl.when((place((x + j + 1) % NX) > place(x)) == above)(functools.partial(signal, semaphore, peer))
 
     def send(src, dst, ss, rs, to):
         copy = pltpu.make_async_remote_copy(
@@ -107,19 +121,29 @@
         signal(barrier, peer)
     q_load = pltpu.make_async_copy(q_hbm, q, load_sem.at[8])
     e_load = pltpu.make_async_copy(e_hbm.at[0], err, load_sem.at[9])
-    loads = {}
-    for k in (2, 1, 3, 0):
-        for t in (1, 0):
-            loads[k, t] = pltpu.make_async_copy(
-                g_hbm.at[0, 0, pl.ds(first_row(k, t), OWN)],
-                g.at[pl.ds(at(k, t), OWN)],
-                load_sem.at[2 * k + t],
-            )
-            loads[k, t].start()
-        if k == 2:
-            signal_far(barrier, True)
-            q_load.start()
-    e_load.start()
+    loads = {
+        (k, t): pltpu.make_async_copy(
+            g_hbm.at[0, 0, pl.ds(first_row(k, t), OWN)],
+            g.at[pl.ds(at(k, t), OWN)],
+            load_sem.at[2 * k + t],
+        )
+        for k in (1, 3, 0)
+        for t in (1, 0)
+    }
+    pieces = {0: (0, CHUNK), 1: (CHUNK, HALF - CHUNK)}
+    far_loads = {
+        (i, t, d): pltpu.make_async_copy(
+            g_hbm.at[0, 0, pl.ds(first_row(2, t) + d * HALF + start, rows)],
+            g.at[pl.ds(at(2, t) + d * HALF + start, rows)],
+            far_sem.at[i, t, d],
+        )
+        for i, (start, rows) in pieces.items()
+        for t in (1, 0)
+        for d in (0, 1)
+    }
+    for load in far_loads.values():
+        load.start()
+    signal_far(barrier, True)
 
     def widen(k, start, rows):
         def step(i, carry):
@@ -145,17 +169,27 @@
 
         lax.fori_loop(0, rows // CHUNK, step, 0)
 
-    loads[2, 1].wait()
-    widen(2, 0, OWN)
-    pl.semaphore_wait(barrier, 3 + z + x + 3 * (x // 2))
+    for d in (0, 1):
+        far_loads[0, 1, d].wait()
+        widen(2, d * HALF, CHUNK)
+    q_load.start()
+    e_load.start()
+    for load in loads.values():
+        load.start()
+    pl.semaphore_wait(barrier, 3 + z + place(x))
 
     order = [(d, i) for i in range(N_CHUNK) for d in (0, 1)]
     copies = {}
-    for d, i in order:
-        copies[d, i] = to_partner(2, d * HALF + i * CHUNK, CHUNK, d * N_CHUNK + i)
-    loads[2, 0].wait()
     far_copies = {}
     for d, i in order:
+        if (d, i) == (0, 1):
+            for e in (0, 1):
+                far_loads[1, 1, e].wait()
+                widen(2, e * HALF + CHUNK, HALF - CHUNK)
+        copies[d, i] = to_partner(2, d * HALF + i * CHUNK, CHUNK, d * N_CHUNK + i)
+    for d, i in order:
+        if i < 2:
+            far_loads[i, 0, d].wait()
         start = d * HALF + i * CHUNK
         copies[d, i].wait_recv()
         add_own(2, start, CHUNK)
@@ -164,17 +198,25 @@
             far.at[d, pl.ds(i * CHUNK, CHUNK)],
             f_ss.at[d, i], f_rs.at[d, i], (up, down)[d],
         )
-
     signal_far(reply, False)
-
-    loads[1, 1].wait()
-    loads[1, 0].wait()
-    widen(1, HALF, HALF)
-    early_up = to_partner(1, HALF, HALF, 8)
-    loads[3, 1].wait()
-    loads[3, 0].wait()
-    widen(3, 0, HALF)
-    early_down = to_partner(3, 0, HALF, 9)
+    for peer in (up, down):
+        signal(ring, peer)
+
+    q_load.wait()
+    qs[pl.ds(0, 3 * RANK), :] = split3(q[...])
+    qs[pl.ds(3 * RANK, RANK), :] = jnp.zeros((RANK, COLS), BF16)
+    e_load.wait()
+
+    def split_error(i, carry):
+        at_row = pl.multiple_of(i * CHUNK, CHUNK)
+        for j, term in enumerate(split(err[pl.ds(at_row, CHUNK), :])):
+            g[pl.ds(ROWS + j * OWN + at_row, CHUNK), :] = term
+        return carry
+
+    lax.fori_loop(0, OWN // CHUNK, split_error, 0)
+    for load in loads.values():
+        load.wait()
+    early = {}
     later = {}
     near_copies = {}
 
@@ -185,11 +227,17 @@
             n_ss.at[d, i], n_rs.at[d, i], (up, down)[d],
         )
 
+    def widen_early():
+        widen(1, HALF, HALF)
+        early[1] = to_partner(1, HALF, HALF, 8)
+        widen(3, 0, HALF)
+        early[3] = to_partner(3, 0, HALF, 9)
+
     def near_early():
-        early_up.wait_recv()
+        early[1].wait_recv()
         add_own(1, HALF, HALF)
         send_near(0, HALF, HALF, N_CHUNK)
-        early_down.wait_recv()
+        early[3].wait_recv()
         add_own(3, 0, HALF)
         send_near(1, 0, HALF, N_CHUNK)
 
@@ -239,7 +287,7 @@
             lax.fori_loop(0, N_CHUNK, step, 0)
 
     def all_reduce(width, bufs, sems, beside):
-        part, core_in, z_in, x_all, y_all, full = bufs
+        part, core_in, z_in, x_all, x_sum, y_all, full = bufs
         ss, rs = sems
         piece = width // NZ
         mine = pl.multiple_of(16 * c, 16)
@@ -271,17 +319,35 @@
         beside("x")
         for copy in copies:
             copy.wait_recv()
-        y_all[y] = (x_all[0] + x_all[1]) + (x_all[2] + x_all[3])
+        total = (x_all[0] + x_all[1]) + (x_all[2] + x_all[3])
+        quartered = y_all.shape[-1] < piece
+        if quartered:
+            quarter = piece // NX
+            x_sum[...] = total
+            y_all[y] = x_sum[:, pl.ds(pl.multiple_of(quarter * x, 128), quarter)]
+            source = x_sum.at[:, pl.ds(pl.multiple_of(quarter * ((x + 2) % NX), 128), quarter)]
+            window = (pl.ds(mine, 16), pl.ds(pl.multiple_of(at_z + quarter * x, 128), quarter))
+        else:
+            y_all[y] = total
+            source = y_all.at[y]
+            window = (pl.ds(mine, 16), pl.ds(at_z, piece))
 
         copies = [
-            send(y_all.at[y], y_all.at[y], ss.at[11 + j], rs.at[11 + j], peer)
+            send(source, y_all.at[y], ss.at[11 + j], rs.at[11 + j], peer)
             for j, peer in enumerate(y_peers)
         ]
         beside("y")
         for copy in copies:
             copy.wait_recv()
-        window = (pl.ds(mine, 16), pl.ds(at_z, piece))
         full[window] = (y_all[0] + y_all[1]) + (y_all[2] + y_all[3])
+        if quartered:
+            copies = [
+                send(full.at[window], full.at[window], ss.at[22 + j], rs.at[22 + j], peer)
+                for j, peer in enumerate(x_peers)
+            ]
+            for copy in copies:
+                copy.wait_recv()
+            window = (pl.ds(mine, 16), pl.ds(at_z, piece))
 
         copies = [
             send(full.at[window], full.at[window], ss.at[14 + j], rs.at[14 + j], peer)
@@ -296,50 +362,58 @@
         beside("core2")
         copy.wait_recv()
 
-    loads[0, 1].wait()
-    loads[0, 0].wait()
-    e_load.wait()
-    q_load.wait()
-    qs[...] = split3(q[...])
     part_f = bufs_f[0]
-    for k in range(NY):
-        terms = fold3(
-            lax.dot_general(qs[...], g[pl.ds(at(k, 0), 2 * OWN), :], NT, preferred_element_type=F32)
-        )
+
+    def left_terms(start, rows):
+        terms = lax.dot_general(
+            g[pl.ds(start, rows), :], qs[...], NT, preferred_element_type=F32
+        )
+        return fold3(terms.T)
+
+    for k in (1, 2, 3):
+        terms = left_terms(at(k, 0), 2 * OWN)
         for t in (0, 1):
-            term = terms[:, OWN * t : OWN * (t + 1)]
-            if (k, t) == (0, 0):
-                term = term + lax.dot_general(
-                    q[...], err[...], NT, precision=HIGHEST, preferred_element_type=F32
-                )
-            part_f[:, pl.ds(first_row(k, t), OWN)] = term
+            part_f[:, pl.ds(first_row(k, t), OWN)] = terms[:, OWN * t : OWN * (t + 1)]
+    terms = left_terms(0, 2 * OWN)
+    own = left_terms(ROWS, 3 * OWN)
+    part_f[:, pl.ds(first_row(0, 1), OWN)] = terms[:, OWN:]
+    part_f[:, pl.ds(first_row(0, 0), OWN)] = (
+        terms[:, :OWN] + own[:, :OWN] + own[:, OWN : 2 * OWN] + own[:, 2 * OWN :]
+    )
 
     def beside_f(phase):
         if phase == "core":
-            near_early()
-            answers = (NZ - 1 - z) + (NX - 1 - x) + 3 * (1 - x // 2)
+            pl.semaphore_wait(ring, 2)
+            answers = (NZ - 1 - z) + (NX - 1 - place(x))
 
             @pl.when(answers > 0)
             def _():
                 pl.semaphore_wait(reply, answers)
+
         elif phase == "z":
+            widen_early()
+        elif phase == "x":
+            near_early()
+        elif phase == "y":
             widen_rest()
         elif phase == "z2":
             near_late()
 
     all_reduce(ROWS, bufs_f, ar_f, beside_f)
-    factor = bufs_f[5]
+    factor = bufs_f[6]
 
     for k in range(NY):
         for t in (0, 1):
             fs[:, pl.ds(at(k, t), OWN)] = split3(factor[:, pl.ds(first_row(k, t), OWN)])
     own_factor = factor[:, pl.ds(first_row(0, 0), OWN)]
+    for j in range(3):
+        fs[:, pl.ds(ROWS + j * OWN, OWN)] = split3(own_factor)
     part_u = bufs_u[0]
     for start in range(0, COLS, 1024):
         cols = pl.ds(start, min(1024, COLS - start))
         part_u[:, cols] = fold3(
             lax.dot_general(fs[...], g[:, cols], NN, preferred_element_type=F32)
-        ) + lax.dot_general(own_factor, err[:, cols], NN, precision=HIGHEST, preferred_element_type=F32)
+        )
     part_u[:, pl.ds(COLS, WIDE - COLS)] = jnp.zeros((RANK, WIDE - COLS), F32)
 
     def beside_u(phase):
@@ -347,11 +421,12 @@
             merge_own()
             whole = factor[...]
             gram = lax.dot_general(whole, whole, NT, precision=HIGHEST, preferred_element_type=F32)
-            linv[...] = inverse_lower(gram)
-        elif phase == "x":
-            basis[...] = lax.dot_general(
-                linv[...], own_factor, NN, precision=HIGHEST, preferred_element_type=F32
+            linv = inverse_lower(gram)
+            linv6[...] = left6((linv * (1.0 / (NX * NZ))).T)
+            basis = lax.dot_general(
+                linv, own_factor, NN, precision=HIGHEST, preferred_element_type=F32
             )
+            basis6[...] = left6(basis)
         elif phase == "z2":
             merge_early()
 
@@ -359,12 +434,10 @@
     for start in range(0, COLS, 1024):
         cols = pl.ds(start, min(1024, COLS - start))
         right = lax.dot_general(
-            linv[...], bufs_u[5][:, cols], NN, precision=HIGHEST, preferred_element_type=F32
-        ) * (1.0 / (NX * NZ))
+            linv6[...], right6(bufs_u[6][:, cols]), NN, preferred_element_type=F32
+        )
         q_next[:, cols] = right
-        value = lax.dot_general(
-            basis[...], right, TN, precision=HIGHEST, preferred_element_type=F32
-        )
+        value = lax.dot_general(basis6[...], right6(right), NN, preferred_element_type=F32)
         approx[:, cols] = value
         new_error[:, cols] -= value
     for i in range(N_CHUNK):
@@ -376,14 +449,15 @@
         copy.wait_send()
 
 
-def reduce_buffers(width):
+def reduce_buffers(width, quartered):
     piece = width // NZ
     return (
         pltpu.VMEM((RANK, width), F32),
         pltpu.VMEM((16, width), F32),
         pltpu.VMEM((NZ - 1, 16, piece), F32),
         pltpu.VMEM((NX, 16, piece), F32),
-        pltpu.VMEM((NY, 16, piece), F32),
+        pltpu.VMEM((16, piece), F32),
+        pltpu.VMEM((NY, 16, piece // NX if quartered else piece), F32),
         pltpu.VMEM((RANK, width), F32),
     )
 
@@ -420,28 +494,30 @@
         in_specs=[any_space] * 3,
         out_specs=(vmem,) * 3,
         scratch_shapes=[
-            pltpu.VMEM((ROWS, COLS), BF16),
+            pltpu.VMEM((ROWS + 3 * OWN, COLS), BF16),
             pltpu.VMEM((OWN, COLS), F32),
             pltpu.VMEM((RANK, COLS), F32),
-            pltpu.VMEM((3 * RANK, COLS), BF16),
+            pltpu.VMEM((4 * RANK, COLS), BF16),
             pltpu.VMEM((NY, OWN, COLS), F32),
             pltpu.VMEM((NY, OWN, COLS), F32),
             pltpu.VMEM((2, HALF, COLS), F32),
             pltpu.VMEM((2, OWN, COLS), F32),
-            pltpu.VMEM((3 * RANK, ROWS), BF16),
-            pltpu.VMEM((RANK, RANK), F32),
-            pltpu.VMEM((RANK, OWN), F32),
-            reduce_buffers(ROWS),
-            reduce_buffers(WIDE),
+            pltpu.VMEM((3 * RANK, ROWS + 3 * OWN), BF16),
+            pltpu.VMEM((RANK, 6 * RANK), BF16),
+            pltpu.VMEM((OWN, 6 * RANK), BF16),
+            reduce_buffers(ROWS, False),
+            reduce_buffers(WIDE, True),
             dma((10,)),
+            dma((2, 2, 2)),
             dma((13,)),
             dma((13,)),
             dma((2, N_CHUNK)),
             dma((2, N_CHUNK)),
             dma((2, N_CHUNK + 1)),
             dma((2, N_CHUNK + 1)),
-            (dma((22,)), dma((22,))),
-            (dma((22,)), dma((22,))),
+            (dma((25,)), dma((25,))),
+            (dma((25,)), dma((25,))),
+            pltpu.SemaphoreType.REGULAR,
             pltpu.SemaphoreType.REGULAR,
         ],
         compiler_params=pltpu.CompilerParams(

time: 79.5 us -> 78.5 us (0.987)
  Pallas kernels: 78.7 us -> 77.8 us
    pallas_call x1, Pallas kernels: 76.5 us -> 75.6 us  [body(): pl.pallas_call(main_kernel, out_shape=(pltpu.VMEM((OWN, COLS), F32), pltp...]
where the time goes in v3:
time: 78.5 us; the launch traced here: 78.4 us
  Pallas kernels  77.8 us (99%)
    pallas_call x1, Pallas kernels, body(): pl.pallas_call(main_kernel, out_shape=(pltpu.VMEM((OWN, COLS), F32), pltp...  75.6 us
    pallas_call x1, Pallas kernels, body(): pl.pallas_call(out_kernel, out_shape=(jax.ShapeDtypeStruct((OWN, COLS), F...  2.2 us

profile of v3, /device:TPU:1, one launch (start us, length us, event | category | flops | bytes accessed | tf_op | source)
XLA Modules:
  0.0 78.4 jit_solution(3320209741653400386)
XLA Ops:
  0.6 75.6 %shard_map.58 = (f32[128,3968]{1,0:T(8,128)S(1)}, f32[128,3968]{1,0:T(8,128)S(1)}, f32[32,3968]{1,0:T(8,128)S(1)}) custom-call(bf16[1,1,1024,3968]{3,2,1,0:T(8,128)(2,1)} %g_hbm.1, f32[1,128,3968]{2,1,0:T(8,128)} %e_hbm.1, f32[32,3968]{1,0:T(8,128)} %q_hbm.1), custom_call_target="tpu_custom_call" | custom-call | flops 2147483648 | bytes 14680064 | tf_op jit(solution)/shard_map/pallas_call | solution.py:487
  76.2 2.2 %shard_map.59 = (f32[128,3968]{1,0:T(8,128)}, f32[1,128,3968]{2,1,0:T(8,128)}, f32[32,3968]{1,0:T(8,128)}) custom-call(f32[128,3968]{1,0:T(8,128)S(1)} %get-tuple-element.6.approx, f32[128,3968]{1,0:T(8,128)S(1)} %get-tuple-element.7.new_error, f32[32,3968]{1,0:T(8,128)S(1)} %get-tuple-element.8.q_next), custom_call_target="tpu_custom_call" | custom-call | tf_op jit(solution)/shard_map/pallas_call | solution.py:530

commit v4 on v3

--- a/solution.py
+++ b/solution.py
@@ -16,8 +16,6 @@
 OWN = 128
 HALF = OWN // 2
 CHUNK = 16
-N_CHUNK = HALF // CHUNK
-N_PART = 4
 WIDE = 4096
 NT = (((1,), (1,)), ((), ()))
 NN = (((1,), (0,)), ((), ()))
@@ -70,7 +68,7 @@
     approx, new_error, q_next,
     g, err, q, qs, psend, precv, far, near, fs, linv6, basis6,
     bufs_f, bufs_u,
-    load_sem, far_sem, p_ss, p_rs, f_ss, f_rs, n_ss, n_rs, ar_f, ar_u, reply, ring,
+    load_sem, sent_sem, p_rs, f_rs, n_rs, ar_f, ar_u, reply, ring_reply, ring,
 ):
     rep, shard = lax.axis_index("rep"), lax.axis_index("shard")
     x, z = rep // NZ, rep % NZ
@@ -87,14 +85,19 @@
     x_peers = [dev(j, 0, 0, 0) for j in range(1, NX)]
     z_peers = [dev(0, 0, j, 0) for j in range(1, NZ)]
     y_peers = [dev(2, j, 0, 0) for j in range(1, NY)]
-    sent = []
     barrier = pltpu.get_barrier_semaphore()
 
     def signal(semaphore, peer):
         pl.semaphore_signal(semaphore, 1, device_id=peer, device_id_type=MESH)
 
-    def place(at_x):
-        return at_x + (at_x == 2) - (at_x == 3)
+    def place(at):
+        return at + (at == 2) - (at == 3)
+
+    def signal_ring(semaphore, above):
+        for j, peer in ((1, up), (3, down)):
+            pl.when((place((y + j) % NY) > place(y)) == above)(
+                functools.partial(signal, semaphore, peer)
+            )
 
     def signal_far(semaphore, above):
         for j, peer in enumerate(z_peers):
@@ -103,13 +106,15 @@
             pl.when((place((x + j + 1) % NX) > place(x)) == above)(functools.partial(signal, semaphore, peer))
 
     def send(src, dst, ss, rs, to):
-        copy = pltpu.make_async_remote_copy(
+        pltpu.make_async_remote_copy(
             src_ref=src, dst_ref=dst, send_sem=ss, recv_sem=rs,
             device_id=to, device_id_type=MESH,
-        )
-        copy.start()
-        sent.append(copy)
-        return copy
+        ).start()
+
+    def wait(semaphore, like):
+        pltpu.make_async_copy(like, like, semaphore).wait()
+
+    to_partner_sent, far_sent, near_sent, sum_sent = (sent_sem.at[i] for i in range(4))
 
     def first_row(k, t):
         return pl.multiple_of(OWN * (2 * ((y + k) % NY) + (c + t) % 2), OWN)
@@ -117,32 +122,19 @@
     def at(k, t):
         return OWN * (2 * k + t)
 
-    for peer in (partner, up, down):
-        signal(barrier, peer)
-    q_load = pltpu.make_async_copy(q_hbm, q, load_sem.at[8])
-    e_load = pltpu.make_async_copy(e_hbm.at[0], err, load_sem.at[9])
-    loads = {
-        (k, t): pltpu.make_async_copy(
-            g_hbm.at[0, 0, pl.ds(first_row(k, t), OWN)],
-            g.at[pl.ds(at(k, t), OWN)],
-            load_sem.at[2 * k + t],
-        )
-        for k in (1, 3, 0)
-        for t in (1, 0)
-    }
-    pieces = {0: (0, CHUNK), 1: (CHUNK, HALF - CHUNK)}
-    far_loads = {
-        (i, t, d): pltpu.make_async_copy(
-            g_hbm.at[0, 0, pl.ds(first_row(2, t) + d * HALF + start, rows)],
-            g.at[pl.ds(at(2, t) + d * HALF + start, rows)],
-            far_sem.at[i, t, d],
-        )
-        for i, (start, rows) in pieces.items()
-        for t in (1, 0)
-        for d in (0, 1)
-    }
-    for load in far_loads.values():
-        load.start()
+    signal(barrier, partner)
+    signal_ring(barrier, True)
+    q_load = pltpu.make_async_copy(q_hbm, q, load_sem.at[0])
+    e_load = pltpu.make_async_copy(e_hbm.at[0], err, load_sem.at[1])
+    for t, start, rows in (
+        (1, 0, CHUNK), (0, 0, CHUNK), (1, CHUNK, HALF - CHUNK), (0, CHUNK, HALF - CHUNK)
+    ):
+        for d in (0, 1):
+            pltpu.make_async_copy(
+                g_hbm.at[0, 0, pl.ds(first_row(2, t) + d * HALF + start, rows)],
+                g.at[pl.ds(at(2, t) + d * HALF + start, rows)],
+                load_sem.at[2 if (t, start) == (1, 0) else 3],
+            ).start()
     signal_far(barrier, True)
 
     def widen(k, start, rows):
@@ -157,7 +149,7 @@
 
     def to_partner(k, start, rows, i):
         window = (k, pl.ds(start, rows))
-        return send(psend.at[window], precv.at[window], p_ss.at[i], p_rs.at[i], partner)
+        send(psend.at[window], precv.at[window], to_partner_sent, p_rs.at[i], partner)
 
     def add_own(k, start, rows):
         def step(i, carry):
@@ -169,35 +161,40 @@
 
         lax.fori_loop(0, rows // CHUNK, step, 0)
 
+    wait(load_sem.at[2], g.at[pl.ds(at(2, 1), 2 * CHUNK)])
     for d in (0, 1):
-        far_loads[0, 1, d].wait()
         widen(2, d * HALF, CHUNK)
     q_load.start()
     e_load.start()
-    for load in loads.values():
-        load.start()
-    pl.semaphore_wait(barrier, 3 + z + place(x))
-
-    order = [(d, i) for i in range(N_CHUNK) for d in (0, 1)]
-    copies = {}
-    far_copies = {}
-    for d, i in order:
-        if (d, i) == (0, 1):
+    for k in (1, 3, 0):
+        for t in (1, 0):
+            pltpu.make_async_copy(
+                g_hbm.at[0, 0, pl.ds(first_row(k, t), OWN)],
+                g.at[pl.ds(at(k, t), OWN)],
+                load_sem.at[4],
+            ).start()
+    below = jnp.minimum(y, NY - y)
+    pl.semaphore_wait(barrier, 1 + below + z + place(x))
+    signal_ring(ring_reply, False)
+
+    pieces = [(d, start, rows) for start, rows in ((0, CHUNK), (CHUNK, HALF - CHUNK)) for d in (0, 1)]
+    for i, (d, start, rows) in enumerate(pieces):
+        if i == 2:
+            wait(load_sem.at[3], g.at[pl.ds(at(2, 0), 2 * OWN - 2 * CHUNK)])
             for e in (0, 1):
-                far_loads[1, 1, e].wait()
                 widen(2, e * HALF + CHUNK, HALF - CHUNK)
-        copies[d, i] = to_partner(2, d * HALF + i * CHUNK, CHUNK, d * N_CHUNK + i)
-    for d, i in order:
-        if i < 2:
-            far_loads[i, 0, d].wait()
-        start = d * HALF + i * CHUNK
-        copies[d, i].wait_recv()
-        add_own(2, start, CHUNK)
-        far_copies[d, i] = send(
-            precv.at[2, pl.ds(start, CHUNK)],
-            far.at[d, pl.ds(i * CHUNK, CHUNK)],
-            f_ss.at[d, i], f_rs.at[d, i], (up, down)[d],
-        )
+        to_partner(2, d * HALF + start, rows, i)
+    for i, (d, start, rows) in enumerate(pieces):
+        here = pl.ds(d * HALF + start, rows)
+        wait(p_rs.at[i], precv.at[2, here])
+        add_own(2, d * HALF + start, rows)
+        if i == 0:
+
+            @pl.when(below < 2)
+            def _():
+                pl.semaphore_wait(ring_reply, 2 - below)
+
+        send(precv.at[2, here], far.at[d, pl.ds(start, rows)], far_sent, f_rs.at[0], (up, down)[d])
     signal_far(reply, False)
     for peer in (up, down):
         signal(ring, peer)
@@ -214,58 +211,63 @@
         return carry
 
     lax.fori_loop(0, OWN // CHUNK, split_error, 0)
-    for load in loads.values():
-        load.wait()
-    early = {}
-    later = {}
-    near_copies = {}
-
+    wait(load_sem.at[4], g.at[pl.ds(0, 3 * 2 * OWN)])
     def send_near(d, start, rows, i):
-        near_copies[d, i] = send(
+        send(
             precv.at[(1, 3)[d], pl.ds(start, rows)],
             near.at[d, pl.ds(start, rows)],
-            n_ss.at[d, i], n_rs.at[d, i], (up, down)[d],
+            near_sent, n_rs.at[i], (up, down)[d],
         )
 
     def widen_early():
         widen(1, HALF, HALF)
-        early[1] = to_partner(1, HALF, HALF, 8)
+        to_partner(1, HALF, HALF, 4)
         widen(3, 0, HALF)
-        early[3] = to_partner(3, 0, HALF, 9)
+        to_partner(3, 0, HALF, 4)
 
     def near_early():
-        early[1].wait_recv()
+        wait(p_rs.at[4], precv.at[0])
         add_own(1, HALF, HALF)
-        send_near(0, HALF, HALF, N_CHUNK)
-        early[3].wait_recv()
+        send_near(0, HALF, HALF, 0)
         add_own(3, 0, HALF)
-        send_near(1, 0, HALF, N_CHUNK)
+        send_near(1, 0, HALF, 0)
 
     def widen_rest():
         widen(1, 0, HALF)
-        later[1] = to_partner(1, 0, HALF, 10)
+        to_partner(1, 0, HALF, 5)
         widen(3, HALF, HALF)
-        later[3] = to_partner(3, HALF, HALF, 11)
+        to_partner(3, HALF, HALF, 5)
         widen(0, 0, OWN)
-        later[0] = to_partner(0, 0, OWN, 12)
+        to_partner(0, 0, OWN, 5)
 
     def near_late():
-        later[1].wait_recv()
-        later[3].wait_recv()
-        for i in range(N_CHUNK):
-            for d, k, start in ((0, 1, 0), (1, 3, HALF)):
-                far_copies[d, i].wait_recv()
-                here = pl.ds(start + i * CHUNK, CHUNK)
-                precv[k, here, :] = (
-                    precv[k, here, :]
-                    + g[pl.ds(at(k, 0) + start + i * CHUNK, CHUNK), :].astype(F32)
-                    + far[d, pl.ds(i * CHUNK, CHUNK), :]
-                )
-                send_near(d, start + i * CHUNK, CHUNK, i)
+        wait(p_rs.at[5], precv.at[pl.ds(0, 2)])
+        wait(f_rs.at[0], far)
+        for i, (first, rows) in enumerate(((0, HALF - CHUNK), (HALF - CHUNK, CHUNK))):
+            for d, k, half in ((0, 1, 0), (1, 3, HALF)):
+
+                def step(j, carry, d=d, k=k, half=half, first=first):
+                    at_row = pl.multiple_of(first + j * CHUNK, CHUNK)
+                    here = pl.ds(half + at_row, CHUNK)
+                    precv[k, here, :] = (
+                        precv[k, here, :]
+                        + g[pl.ds(at(k, 0) + half + at_row, CHUNK), :].astype(F32)
+                        + far[d, pl.ds(at_row, CHUNK), :]
+                    )
+                    return carry
+
+                lax.fori_loop(0, rows // CHUNK, step, 0)
+                send_near(d, half + first, rows, 1 + i)
+
+    def add_near(d, start, rows):
+        def step(j, carry):
+            here = pl.ds(pl.multiple_of(start + j * CHUNK, CHUNK), CHUNK)
+            new_error[here, :] += near[d, here, :]
+            return carry
+
+        lax.fori_loop(0, rows // CHUNK, step, 0)
 
     def merge_own():
-        later[0].wait_recv()
-
         def step(i, carry):
             here = pl.ds(pl.multiple_of(i * CHUNK, CHUNK), CHUNK)
             new_error[here, :] = (
@@ -276,49 +278,40 @@
         lax.fori_loop(0, OWN // CHUNK, step, 0)
 
     def merge_early():
-        for d, start in ((0, HALF), (1, 0)):
-            near_copies[d, N_CHUNK].wait_recv()
-
-            def step(j, carry, d=d, start=start):
-                here = pl.ds(pl.multiple_of(start + j * CHUNK, CHUNK), CHUNK)
-                new_error[here, :] += near[d, here, :]
-                return carry
-
-            lax.fori_loop(0, N_CHUNK, step, 0)
+        wait(n_rs.at[0], near.at[0])
+        add_near(0, HALF, HALF)
+        add_near(1, 0, HALF)
 
     def all_reduce(width, bufs, sems, beside):
         part, core_in, z_in, x_all, x_sum, y_all, full = bufs
-        ss, rs = sems
         piece = width // NZ
         mine = pl.multiple_of(16 * c, 16)
         theirs = pl.multiple_of(16 * (1 - c), 16)
         at_z = pl.multiple_of(piece * z, 128)
 
-        copy = send(part.at[pl.ds(theirs, 16)], core_in, ss.at[0], rs.at[0], partner)
-        beside("core")
-        copy.wait_recv()
+        def phase(name, i, copies, like):
+            for src, dst, peer in copies:
+                send(src, dst, sum_sent, sems.at[i], peer)
+            beside(name)
+            wait(sems.at[i], like)
+            wait(sum_sent, like)
+
+        phase("core", 0, [(part.at[pl.ds(theirs, 16)], core_in, partner)], core_in)
         core_in[...] += part[pl.ds(mine, 16), :]
 
-        copies = []
-        for j, peer in enumerate(z_peers):
-            there = pl.multiple_of(piece * ((z + j + 1) % NZ), 128)
-            copies.append(
-                send(core_in.at[:, pl.ds(there, piece)], z_in.at[j], ss.at[1 + j], rs.at[1 + j], peer)
-            )
-        beside("z")
+        def there(j):
+            return pl.ds(pl.multiple_of(piece * ((z + j + 1) % NZ), 128), piece)
+
+        phase(
+            "z", 1, [(core_in.at[:, there(j)], z_in.at[j], peer) for j, peer in enumerate(z_peers)], z_in
+        )
         total = core_in[:, pl.ds(at_z, piece)]
-        for j, copy in enumerate(copies):
-            copy.wait_recv()
+        for j in range(NZ - 1):
             total = total + z_in[j]
         x_all[x] = total
-
-        copies = [
-            send(x_all.at[x], x_all.at[x], ss.at[8 + j], rs.at[8 + j], peer)
-            for j, peer in enumerate(x_peers)
-        ]
-        beside("x")
-        for copy in copies:
-            copy.wait_recv()
+        phase(
+            "x", 2, [(x_all.at[x], x_all.at[x], peer) for peer in x_peers], x_all.at[pl.ds(0, NX - 1)]
+        )
         total = (x_all[0] + x_all[1]) + (x_all[2] + x_all[3])
         quartered = y_all.shape[-1] < piece
         if quartered:
@@ -331,36 +324,15 @@
             y_all[y] = total
             source = y_all.at[y]
             window = (pl.ds(mine, 16), pl.ds(at_z, piece))
-
-        copies = [
-            send(source, y_all.at[y], ss.at[11 + j], rs.at[11 + j], peer)
-            for j, peer in enumerate(y_peers)
-        ]
-        beside("y")
-        for copy in copies:
-            copy.wait_recv()
+        three = y_all.at[pl.ds(0, NY - 1)]
+        phase("y", 3, [(source, y_all.at[y], peer) for peer in y_peers], three)
         full[window] = (y_all[0] + y_all[1]) + (y_all[2] + y_all[3])
         if quartered:
-            copies = [
-                send(full.at[window], full.at[window], ss.at[22 + j], rs.at[22 + j], peer)
-                for j, peer in enumerate(x_peers)
-            ]
-            for copy in copies:
-                copy.wait_recv()
+            phase("x2", 4, [(full.at[window], full.at[window], peer) for peer in x_peers], three)
             window = (pl.ds(mine, 16), pl.ds(at_z, piece))
-
-        copies = [
-            send(full.at[window], full.at[window], ss.at[14 + j], rs.at[14 + j], peer)
-            for j, peer in enumerate(z_peers)
-        ]
-        beside("z2")
-        for copy in copies:
-            copy.wait_recv()
-
+        phase("z2", 5, [(full.at[window], full.at[window], peer) for peer in z_peers], z_in)
         window = (pl.ds(mine, 16),)
-        copy = send(full.at[window], full.at[window], ss.at[21], rs.at[21], partner)
-        beside("core2")
-        copy.wait_recv()
+        phase("core2", 6, [(full.at[window], full.at[window], partner)], core_in)
 
     part_f = bufs_f[0]
 
@@ -440,13 +412,13 @@
         value = lax.dot_general(basis6[...], right6(right), NN, preferred_element_type=F32)
         approx[:, cols] = value
         new_error[:, cols] -= value
-    for i in range(N_CHUNK):
-        for d, start in ((0, 0), (1, HALF)):
-            near_copies[d, i].wait_recv()
-            here = pl.ds(start + i * CHUNK, CHUNK)
-            new_error[here, :] += near[d, here, :]
-    for copy in sent:
-        copy.wait_send()
+    wait(to_partner_sent, psend)
+    wait(far_sent, far)
+    for i, first, rows in ((1, 0, HALF - CHUNK), (2, HALF - CHUNK, CHUNK)):
+        wait(n_rs.at[i], near.at[0, pl.ds(0, 2 * rows)])
+        add_near(0, first, rows)
+        add_near(1, HALF + first, rows)
+    wait(near_sent, near)
 
 
 def reduce_buffers(width, quartered):
@@ -463,17 +435,11 @@
 
 
 def out_kernel(approx, new_error, q_next, approx_out, new_error_out, q_out, sem):
-    copies = [pltpu.make_async_copy(q_next, q_out, sem.at[0])]
-    for i in range(N_PART):
-        rows = pl.ds(i * (OWN // N_PART), OWN // N_PART)
-        copies.append(
-            pltpu.make_async_copy(approx.at[rows], approx_out.at[rows], sem.at[1 + 2 * i])
-        )
-        copies.append(
-            pltpu.make_async_copy(
-                new_error.at[rows], new_error_out.at[0, rows], sem.at[2 + 2 * i]
-            )
-        )
+    copies = [
+        pltpu.make_async_copy(approx, approx_out, sem.at[0]),
+        pltpu.make_async_copy(new_error, new_error_out.at[0], sem.at[1]),
+        pltpu.make_async_copy(q_next, q_out, sem.at[2]),
+    ]
     for copy in copies:
         copy.start()
     for copy in copies:
@@ -507,16 +473,14 @@
             pltpu.VMEM((OWN, 6 * RANK), BF16),
             reduce_buffers(ROWS, False),
             reduce_buffers(WIDE, True),
-            dma((10,)),
-            dma((2, 2, 2)),
-            dma((13,)),
-            dma((13,)),
-            dma((2, N_CHUNK)),
-            dma((2, N_CHUNK)),
-            dma((2, N_CHUNK + 1)),
-            dma((2, N_CHUNK + 1)),
-            (dma((25,)), dma((25,))),
-            (dma((25,)), dma((25,))),
+            dma((5,)),
+            dma((4,)),
+            dma((6,)),
+            dma((1,)),
+            dma((3,)),
+            dma((7,)),
+            dma((7,)),
+            pltpu.SemaphoreType.REGULAR,
             pltpu.SemaphoreType.REGULAR,
             pltpu.SemaphoreType.REGULAR,
         ],
@@ -536,7 +500,7 @@
         ),
         in_specs=[vmem] * 3,
         out_specs=(any_space,) * 3,
-        scratch_shapes=[dma((1 + 2 * N_PART,))],
+        scratch_shapes=[dma((3,))],
         compiler_params=pltpu.CompilerParams(vmem_limit_bytes=16 << 20),
     )(*results)
 

time: 78.5 us -> 77 us (0.981)
  Pallas kernels: 77.8 us -> 76.3 us
    pallas_call x1, Pallas kernels: 75.6 us -> 74.1 us  [body(): pl.pallas_call(main_kernel, out_shape=(pltpu.VMEM((OWN, COLS), F32), pltp...]
where the time goes in v4:
time: 77 us; the launch traced here: 76.9 us
  Pallas kernels  76.3 us (99%)
    pallas_call x1, Pallas kernels, body(): pl.pallas_call(main_kernel, out_shape=(pltpu.VMEM((OWN, COLS), F32), pltp...  74.1 us
    pallas_call x1, Pallas kernels, body(): pl.pallas_call(out_kernel, out_shape=(jax.ShapeDtypeStruct((OWN, COLS), F...  2.15 us

profile of v4, /device:TPU:1, one launch (start us, length us, event | category | flops | bytes accessed | tf_op | source)
XLA Modules:
  0.0 76.9 jit_solution(5708634669706532141)
XLA Ops:
  0.6 74.1 %shard_map.58 = (f32[128,3968]{1,0:T(8,128)S(1)}, f32[128,3968]{1,0:T(8,128)S(1)}, f32[32,3968]{1,0:T(8,128)S(1)}) custom-call(bf16[1,1,1024,3968]{3,2,1,0:T(8,128)(2,1)} %g_hbm.1, f32[1,128,3968]{2,1,0:T(8,128)} %e_hbm.1, f32[32,3968]{1,0:T(8,128)} %q_hbm.1), custom_call_target="tpu_custom_call" | custom-call | flops 2147483648 | bytes 14680064 | tf_op jit(solution)/shard_map/pallas_call | solution.py:453
  74.8 2.1 %shard_map.59 = (f32[128,3968]{1,0:T(8,128)}, f32[1,128,3968]{2,1,0:T(8,128)}, f32[32,3968]{1,0:T(8,128)}) custom-call(f32[128,3968]{1,0:T(8,128)S(1)} %get-tuple-element.6.approx, f32[128,3968]{1,0:T(8,128)S(1)} %get-tuple-element.7.new_error, f32[32,3968]{1,0:T(8,128)S(1)} %get-tuple-element.8.q_next), custom_call_target="tpu_custom_call" | custom-call | tf_op jit(solution)/shard_map/pallas_call | solution.py:494

commit v5 on v4

--- a/solution.py
+++ b/solution.py
@@ -16,6 +16,11 @@
 OWN = 128
 HALF = OWN // 2
 CHUNK = 16
+FIRST = 1024
+LAST = ((0, HALF - 8), (HALF - 8, 8))
+CORNER = 640
+FULL = COLS - CORNER
+CORNER_ROWS = (HALF - CHUNK, HALF)
 WIDE = 4096
 NT = (((1,), (1,)), ((), ()))
 NN = (((1,), (0,)), ((), ()))
@@ -66,7 +71,7 @@
 def main_kernel(
     g_hbm, e_hbm, q_hbm,
     approx, new_error, q_next,
-    g, err, q, qs, psend, precv, far, near, fs, linv6, basis6,
+    g, err, q, qs, psend, precv, far, corner, near, fs, linv6, basis6,
     bufs_f, bufs_u,
     load_sem, sent_sem, p_rs, f_rs, n_rs, ar_f, ar_u, reply, ring_reply, ring,
 ):
@@ -114,7 +119,9 @@
     def wait(semaphore, like):
         pltpu.make_async_copy(like, like, semaphore).wait()
 
-    to_partner_sent, far_sent, near_sent, sum_sent = (sent_sem.at[i] for i in range(4))
+    but_corners = psend.at[pl.ds(0, 2), pl.ds(0, 112), pl.ds(0, 17 * 128)]
+
+    to_partner_sent, far_sent, corner_sent, near_sent, sum_sent = (sent_sem.at[i] for i in range(5))
 
     def first_row(k, t):
         return pl.multiple_of(OWN * (2 * ((y + k) % NY) + (c + t) % 2), OWN)
@@ -123,19 +130,27 @@
         return OWN * (2 * k + t)
 
     signal(barrier, partner)
+    corner[...] = jnp.zeros(corner.shape, F32)
+    for d in (0, 1):
+        far[d, pl.ds((1 - d) * (HALF - CHUNK), CHUNK), pl.ds(FULL, CORNER)] = jnp.zeros(
+            (CHUNK, CORNER), F32
+        )
     signal_ring(barrier, True)
     q_load = pltpu.make_async_copy(q_hbm, q, load_sem.at[0])
     e_load = pltpu.make_async_copy(e_hbm.at[0], err, load_sem.at[1])
-    for t, start, rows in (
-        (1, 0, CHUNK), (0, 0, CHUNK), (1, CHUNK, HALF - CHUNK), (0, CHUNK, HALF - CHUNK)
-    ):
+    def load_far(t, start, rows, i):
         for d in (0, 1):
             pltpu.make_async_copy(
                 g_hbm.at[0, 0, pl.ds(first_row(2, t) + d * HALF + start, rows)],
                 g.at[pl.ds(at(2, t) + d * HALF + start, rows)],
-                load_sem.at[2 if (t, start) == (1, 0) else 3],
+                load_sem.at[i],
             ).start()
+
+    load_far(1, 0, CHUNK, 2)
     signal_far(barrier, True)
+    load_far(0, 0, CHUNK, 3)
+    load_far(1, CHUNK, HALF - CHUNK, 3)
+    load_far(0, CHUNK, HALF - CHUNK, 3)
 
     def widen(k, start, rows):
         def step(i, carry):
@@ -147,15 +162,15 @@
 
         lax.fori_loop(0, rows // CHUNK, step, 0)
 
-    def to_partner(k, start, rows, i):
-        window = (k, pl.ds(start, rows))
+    def to_partner(k, start, rows, i, cols=slice(None)):
+        window = (k, pl.ds(start, rows), cols)
         send(psend.at[window], precv.at[window], to_partner_sent, p_rs.at[i], partner)
 
-    def add_own(k, start, rows):
+    def add_own(k, start, rows, cols=slice(None)):
         def step(i, carry):
             at_row = pl.multiple_of(start + i * CHUNK, CHUNK)
-            precv[k, pl.ds(at_row, CHUNK), :] += g[
-                pl.ds(at(k, 0) + at_row, CHUNK), :
+            precv[k, pl.ds(at_row, CHUNK), cols] += g[
+                pl.ds(at(k, 0) + at_row, CHUNK), cols
             ].astype(F32)
             return carry
 
@@ -177,24 +192,48 @@
     pl.semaphore_wait(barrier, 1 + below + z + place(x))
     signal_ring(ring_reply, False)
 
-    pieces = [(d, start, rows) for start, rows in ((0, CHUNK), (CHUNK, HALF - CHUNK)) for d in (0, 1)]
-    for i, (d, start, rows) in enumerate(pieces):
-        if i == 2:
+    few, most, every = pl.ds(0, FIRST), pl.ds(FIRST, COLS - FIRST), pl.ds(0, COLS)
+    pieces = [
+        (d, start, rows, cols)
+        for start, rows, cols in (
+            (0, CHUNK, few), (0, CHUNK, most), (CHUNK, HALF - CHUNK, every)
+        )
+        for d in (0, 1)
+    ]
+    tails = [pl.ds(FULL, CORNER), pl.ds(0, FULL)]
+    own_way = {
+        3: [(0, CHUNK, pl.ds(FIRST, FULL - FIRST))],
+        4: [(CHUNK, HALF - 2 * CHUNK, every), (HALF - CHUNK, CHUNK, tails[1])],
+    }
+    for i, (d, start, rows, cols) in enumerate(pieces):
+        if i == 4:
             wait(load_sem.at[3], g.at[pl.ds(at(2, 0), 2 * OWN - 2 * CHUNK)])
             for e in (0, 1):
                 widen(2, e * HALF + CHUNK, HALF - CHUNK)
-        to_partner(2, d * HALF + start, rows, i)
-    for i, (d, start, rows) in enumerate(pieces):
-        here = pl.ds(d * HALF + start, rows)
-        wait(p_rs.at[i], precv.at[2, here])
-        add_own(2, d * HALF + start, rows)
+        to_partner(2, d * HALF + start, rows, i, cols)
+    for i, (d, start, rows, cols) in enumerate(pieces):
+        here = (2, pl.ds(d * HALF + start, rows), cols)
+        wait(p_rs.at[i], precv.at[here])
+        add_own(2, d * HALF + start, rows, cols)
         if i == 0:
 
             @pl.when(below < 2)
             def _():
                 pl.semaphore_wait(ring_reply, 2 - below)
 
-        send(precv.at[2, here], far.at[d, pl.ds(start, rows)], far_sent, f_rs.at[0], (up, down)[d])
+        for start, rows, cols in own_way.get(i, [(start, rows, cols)]):
+            send(
+                precv.at[2, pl.ds(d * HALF + start, rows), cols],
+                far.at[d, pl.ds(start, rows), cols], far_sent, f_rs.at[0], (up, down)[d],
+            )
+    for r, odd in ((0, 3), (1, 1)):
+        source = precv.at[2, pl.ds(CORNER_ROWS[r], CHUNK), tails[0]]
+        for way in (0, 1):
+
+            @pl.when((y == odd) == (way != r))
+            def _(r=r, way=way, source=source):
+                send(source, corner.at[way, r], corner_sent, f_rs.at[1], (up, down)[way])
+
     signal_far(reply, False)
     for peer in (up, down):
         signal(ring, peer)
@@ -212,60 +251,78 @@
 
     lax.fori_loop(0, OWN // CHUNK, split_error, 0)
     wait(load_sem.at[4], g.at[pl.ds(0, 3 * 2 * OWN)])
-    def send_near(d, start, rows, i):
+    def send_near(d, start, rows, i, cols=slice(None)):
+        window = (pl.ds(start, rows), cols)
         send(
-            precv.at[(1, 3)[d], pl.ds(start, rows)],
-            near.at[d, pl.ds(start, rows)],
+            precv.at[((1, 3)[d], *window)],
+            near.at[(d, *window)],
             near_sent, n_rs.at[i], (up, down)[d],
         )
 
     def widen_early():
         widen(1, HALF, HALF)
-        to_partner(1, HALF, HALF, 4)
+        to_partner(1, HALF, HALF, 6)
         widen(3, 0, HALF)
-        to_partner(3, 0, HALF, 4)
+        to_partner(3, 0, HALF, 6)
 
     def near_early():
-        wait(p_rs.at[4], precv.at[0])
+        wait(p_rs.at[6], precv.at[0])
         add_own(1, HALF, HALF)
-        send_near(0, HALF, HALF, 0)
+        send_near(0, HALF + CHUNK, HALF - CHUNK, 0)
+        send_near(0, HALF, CHUNK, 0, tails[1])
         add_own(3, 0, HALF)
-        send_near(1, 0, HALF, 0)
+        send_near(1, 0, HALF - CHUNK, 0)
+        send_near(1, HALF - CHUNK, CHUNK, 0, tails[1])
 
     def widen_rest():
         widen(1, 0, HALF)
-        to_partner(1, 0, HALF, 5)
+        to_partner(1, 0, HALF, 7)
         widen(3, HALF, HALF)
-        to_partner(3, HALF, HALF, 5)
+        to_partner(3, HALF, HALF, 7)
         widen(0, 0, OWN)
-        to_partner(0, 0, OWN, 5)
+        to_partner(0, 0, OWN, 7)
 
     def near_late():
-        wait(p_rs.at[5], precv.at[pl.ds(0, 2)])
-        wait(f_rs.at[0], far)
-        for i, (first, rows) in enumerate(((0, HALF - CHUNK), (HALF - CHUNK, CHUNK))):
-            for d, k, half in ((0, 1, 0), (1, 3, HALF)):
-
-                def step(j, carry, d=d, k=k, half=half, first=first):
-                    at_row = pl.multiple_of(first + j * CHUNK, CHUNK)
-                    here = pl.ds(half + at_row, CHUNK)
-                    precv[k, here, :] = (
-                        precv[k, here, :]
-                        + g[pl.ds(at(k, 0) + half + at_row, CHUNK), :].astype(F32)
-                        + far[d, pl.ds(at_row, CHUNK), :]
-                    )
-                    return carry
-
-                lax.fori_loop(0, rows // CHUNK, step, 0)
+        wait(p_rs.at[7], precv.at[pl.ds(0, 2)])
+        wait(f_rs.at[0], but_corners)
+
+        @pl.when(y % 2 == 1)
+        def _():
+            wait(f_rs.at[1], corner.at[0])
+
+        @pl.when(y == 2)
+        def _():
+            wait(f_rs.at[1], corner)
+
+        for d, k in ((0, 1), (1, 3)):
+            for r in (0, 1):
+                here = (k, pl.ds(CORNER_ROWS[r], CHUNK), tails[0])
+                precv[here] += corner[d, r]
+            send_near(d, CORNER_ROWS[1 - d], CHUNK, 3, tails[0])
+        for d, k, half in ((0, 1, 0), (1, 3, HALF)):
+
+            def step(j, carry, d=d, k=k, half=half):
+                at_row = pl.multiple_of(j * CHUNK, CHUNK)
+                here = pl.ds(half + at_row, CHUNK)
+                precv[k, here, :] = (
+                    precv[k, here, :]
+                    + g[pl.ds(at(k, 0) + half + at_row, CHUNK), :].astype(F32)
+                    + far[d, pl.ds(at_row, CHUNK), :]
+                )
+                return carry
+
+            lax.fori_loop(0, HALF // CHUNK, step, 0)
+        for i, (first, rows) in enumerate(LAST):
+            for d, half in ((0, 0), (1, HALF)):
                 send_near(d, half + first, rows, 1 + i)
 
     def add_near(d, start, rows):
         def step(j, carry):
-            here = pl.ds(pl.multiple_of(start + j * CHUNK, CHUNK), CHUNK)
+            here = pl.ds(pl.multiple_of(start + j * 8, 8), 8)
             new_error[here, :] += near[d, here, :]
             return carry
 
-        lax.fori_loop(0, rows // CHUNK, step, 0)
+        lax.fori_loop(0, rows // 8, step, 0)
 
     def merge_own():
         def step(i, carry):
@@ -278,7 +335,8 @@
         lax.fori_loop(0, OWN // CHUNK, step, 0)
 
     def merge_early():
-        wait(n_rs.at[0], near.at[0])
+        wait(n_rs.at[0], but_corners)
+        wait(n_rs.at[3], corner.at[0])
         add_near(0, HALF, HALF)
         add_near(1, 0, HALF)
 
@@ -413,9 +471,10 @@
         approx[:, cols] = value
         new_error[:, cols] -= value
     wait(to_partner_sent, psend)
-    wait(far_sent, far)
-    for i, first, rows in ((1, 0, HALF - CHUNK), (2, HALF - CHUNK, CHUNK)):
-        wait(n_rs.at[i], near.at[0, pl.ds(0, 2 * rows)])
+    wait(far_sent, but_corners)
+    wait(corner_sent, corner.at[0])
+    for i, (first, rows) in enumerate(LAST):
+        wait(n_rs.at[1 + i], near.at[0, pl.ds(0, 2 * rows)])
         add_near(0, first, rows)
         add_near(1, HALF + first, rows)
     wait(near_sent, near)
@@ -467,6 +526,7 @@
             pltpu.VMEM((NY, OWN, COLS), F32),
             pltpu.VMEM((NY, OWN, COLS), F32),
             pltpu.VMEM((2, HALF, COLS), F32),
+            pltpu.VMEM((2, 2, CHUNK, CORNER), F32),
             pltpu.VMEM((2, OWN, COLS), F32),
             pltpu.VMEM((3 * RANK, ROWS + 3 * OWN), BF16),
             pltpu.VMEM((RANK, 6 * RANK), BF16),
@@ -474,10 +534,10 @@
             reduce_buffers(ROWS, False),
             reduce_buffers(WIDE, True),
             dma((5,)),
+            dma((5,)),
+            dma((8,)),
+            dma((2,)),
             dma((4,)),
-            dma((6,)),
-            dma((1,)),
-            dma((3,)),
             dma((7,)),
             dma((7,)),
             pltpu.SemaphoreType.REGULAR,

time: 77 us -> 76.1 us (0.988)
  Pallas kernels: 76.3 us -> 75.4 us
    pallas_call x1, Pallas kernels: 74.1 us -> 73.3 us  [body(): pl.pallas_call(main_kernel, out_shape=(pltpu.VMEM((OWN, COLS), F32), pltp...]
where the time goes in v5:
time: 76.1 us; the launch traced here: 76 us
  Pallas kernels  75.4 us (99%)
    pallas_call x1, Pallas kernels, body(): pl.pallas_call(main_kernel, out_shape=(pltpu.VMEM((OWN, COLS), F32), pltp...  73.3 us
    pallas_call x1, Pallas kernels, body(): pl.pallas_call(out_kernel, out_shape=(jax.ShapeDtypeStruct((OWN, COLS), F...  2.15 us

profile of v5, /device:TPU:1, one launch (start us, length us, event | category | flops | bytes accessed | tf_op | source)
XLA Modules:
  0.0 76.0 jit_solution(11190544062038661653)
XLA Ops:
  0.6 73.3 %shard_map.58 = (f32[128,3968]{1,0:T(8,128)S(1)}, f32[128,3968]{1,0:T(8,128)S(1)}, f32[32,3968]{1,0:T(8,128)S(1)}) custom-call(bf16[1,1,1024,3968]{3,2,1,0:T(8,128)(2,1)} %g_hbm.1, f32[1,128,3968]{2,1,0:T(8,128)} %e_hbm.1, f32[32,3968]{1,0:T(8,128)} %q_hbm.1), custom_call_target="tpu_custom_call" | custom-call | flops 2147483648 | bytes 14680064 | tf_op jit(solution)/shard_map/pallas_call | solution.py:512
  73.9 2.1 %shard_map.59 = (f32[128,3968]{1,0:T(8,128)}, f32[1,128,3968]{2,1,0:T(8,128)}, f32[32,3968]{1,0:T(8,128)}) custom-call(f32[128,3968]{1,0:T(8,128)S(1)} %get-tuple-element.6.approx, f32[128,3968]{1,0:T(8,128)S(1)} %get-tuple-element.7.new_error, f32[32,3968]{1,0:T(8,128)S(1)} %get-tuple-element.8.q_next), custom_call_target="tpu_custom_call" | custom-call | tf_op jit(solution)/shard_map/pallas_call | solution.py:554

commit v6 on v5

--- a/solution.py
+++ b/solution.py
@@ -73,7 +73,7 @@
     approx, new_error, q_next,
     g, err, q, qs, psend, precv, far, corner, near, fs, linv6, basis6,
     bufs_f, bufs_u,
-    load_sem, sent_sem, p_rs, f_rs, n_rs, ar_f, ar_u, reply, ring_reply, ring,
+    load_sem, sent_sem, p_rs, f_rs, n_rs, ar_f, ar_u, reply, known, ring_reply, ring,
 ):
     rep, shard = lax.axis_index("rep"), lax.axis_index("shard")
     x, z = rep // NZ, rep % NZ
@@ -89,7 +89,7 @@
     up, down = dev(0, 1, 0, 0), dev(0, NY - 1, 0, 0)
     x_peers = [dev(j, 0, 0, 0) for j in range(1, NX)]
     z_peers = [dev(0, 0, j, 0) for j in range(1, NZ)]
-    y_peers = [dev(2, j, 0, 0) for j in range(1, NY)]
+    y_peers = [dev(1, j, 0, 0) for j in range(1, NY)]
     barrier = pltpu.get_barrier_semaphore()
 
     def signal(semaphore, peer):
@@ -106,7 +106,14 @@
 
     def signal_far(semaphore, above):
         for j, peer in enumerate(z_peers):
-            pl.when((z + j + 1 < NZ) == above)(functools.partial(signal, semaphore, peer))
+            greets = (z + j + 1 < NZ) == above
+            if j == 2:
+                greets = greets & (z != 4)
+            elif j == 3:
+                greets = greets & (z % 4 != 3)
+            elif j == 4:
+                greets = greets & (z != NZ - 1)
+            pl.when(greets)(functools.partial(signal, semaphore, peer))
         for j, peer in enumerate(x_peers):
             pl.when((place((x + j + 1) % NX) > place(x)) == above)(functools.partial(signal, semaphore, peer))
 
@@ -189,7 +196,8 @@
                 load_sem.at[4],
             ).start()
     below = jnp.minimum(y, NY - y)
-    pl.semaphore_wait(barrier, 1 + below + z + place(x))
+    below_z = z - 2 * (z // (NZ - 1))
+    pl.semaphore_wait(barrier, 1 + below + below_z + place(x))
     signal_ring(ring_reply, False)
 
     few, most, every = pl.ds(0, FIRST), pl.ds(FIRST, COLS - FIRST), pl.ds(0, COLS)
@@ -251,6 +259,14 @@
 
     lax.fori_loop(0, OWN // CHUNK, split_error, 0)
     wait(load_sem.at[4], g.at[pl.ds(0, 3 * 2 * OWN)])
+    answers = (NZ - 1 - z) - ((z == 3) | (z == 4)) + (NX - 1 - place(x))
+
+    @pl.when(z == NZ - 2)
+    def _():
+        pl.semaphore_wait(reply, answers)
+        for j in (1, NZ - 2, NZ - 3):
+            signal(known, z_peers[j - 1])
+
     def send_near(d, start, rows, i, cols=slice(None)):
         window = (pl.ds(start, rows), cols)
         send(
@@ -376,7 +392,7 @@
             quarter = piece // NX
             x_sum[...] = total
             y_all[y] = x_sum[:, pl.ds(pl.multiple_of(quarter * x, 128), quarter)]
-            source = x_sum.at[:, pl.ds(pl.multiple_of(quarter * ((x + 2) % NX), 128), quarter)]
+            source = x_sum.at[:, pl.ds(pl.multiple_of(quarter * ((x + 1) % NX), 128), quarter)]
             window = (pl.ds(mine, 16), pl.ds(pl.multiple_of(at_z + quarter * x, 128), quarter))
         else:
             y_all[y] = total
@@ -414,11 +430,13 @@
     def beside_f(phase):
         if phase == "core":
             pl.semaphore_wait(ring, 2)
-            answers = (NZ - 1 - z) + (NX - 1 - place(x))
-
-            @pl.when(answers > 0)
+            @pl.when((answers > 0) & (z != NZ - 2))
             def _():
                 pl.semaphore_wait(reply, answers)
+
+            @pl.when((z == 3) | (z == 4) | (z == NZ - 1))
+            def _():
+                pl.semaphore_wait(known, 1)
 
         elif phase == "z":
             widen_early()
@@ -543,6 +561,7 @@
             pltpu.SemaphoreType.REGULAR,
             pltpu.SemaphoreType.REGULAR,
             pltpu.SemaphoreType.REGULAR,
+            pltpu.SemaphoreType.REGULAR,
         ],
         compiler_params=pltpu.CompilerParams(
             collective_id=0, has_side_effects=True, vmem_limit_bytes=48 << 20

time: 76.1 us -> 76.1 us (level)
  no operation moved by 1% of the time
where the time goes in v6:
time: 76.1 us; the launch traced here: 76 us
  Pallas kernels  75.4 us (99%)
    pallas_call x1, Pallas kernels, body(): pl.pallas_call(main_kernel, out_shape=(pltpu.VMEM((OWN, COLS), F32), pltp...  73.3 us
    pallas_call x1, Pallas kernels, body(): pl.pallas_call(out_kernel, out_shape=(jax.ShapeDtypeStruct((OWN, COLS), F...  2.15 us

profile of v6, /device:TPU:1, one launch (start us, length us, event | category | flops | bytes accessed | tf_op | source)
XLA Modules:
  0.0 76.0 jit_solution(14532364849754247487)
XLA Ops:
  0.6 73.3 %shard_map.58 = (f32[128,3968]{1,0:T(8,128)S(1)}, f32[128,3968]{1,0:T(8,128)S(1)}, f32[32,3968]{1,0:T(8,128)S(1)}) custom-call(bf16[1,1,1024,3968]{3,2,1,0:T(8,128)(2,1)} %g_hbm.1, f32[1,128,3968]{2,1,0:T(8,128)} %e_hbm.1, f32[32,3968]{1,0:T(8,128)} %q_hbm.1), custom_call_target="tpu_custom_call" | custom-call | flops 2147483648 | bytes 14680064 | tf_op jit(solution)/shard_map/pallas_call | solution.py:530
  73.9 2.1 %shard_map.59 = (f32[128,3968]{1,0:T(8,128)}, f32[1,128,3968]{2,1,0:T(8,128)}, f32[32,3968]{1,0:T(8,128)}) custom-call(f32[128,3968]{1,0:T(8,128)S(1)} %get-tuple-element.6.approx, f32[128,3968]{1,0:T(8,128)S(1)} %get-tuple-element.7.new_error, f32[32,3968]{1,0:T(8,128)S(1)} %get-tuple-element.8.q_next), custom_call_target="tpu_custom_call" | custom-call | tf_op jit(solution)/shard_map/pallas_call | solution.py:573

commit v7 on v6

--- a/solution.py
+++ b/solution.py
@@ -18,7 +18,7 @@
 CHUNK = 16
 FIRST = 1024
 LAST = ((0, HALF - 8), (HALF - 8, 8))
-CORNER = 640
+CORNER = 768
 FULL = COLS - CORNER
 CORNER_ROWS = (HALF - CHUNK, HALF)
 WIDE = 4096
@@ -126,9 +126,9 @@
     def wait(semaphore, like):
         pltpu.make_async_copy(like, like, semaphore).wait()
 
-    but_corners = psend.at[pl.ds(0, 2), pl.ds(0, 112), pl.ds(0, 17 * 128)]
-
-    to_partner_sent, far_sent, corner_sent, near_sent, sum_sent = (sent_sem.at[i] for i in range(5))
+    but_corners = g.at[pl.ds(0, 59 * 16), pl.ds(0, 8 * 128)]
+
+    to_partner_sent, ring_sent, sum_sent = (sent_sem.at[i] for i in range(3))
 
     def first_row(k, t):
         return pl.multiple_of(OWN * (2 * ((y + k) % NY) + (c + t) % 2), OWN)
@@ -232,7 +232,7 @@
         for start, rows, cols in own_way.get(i, [(start, rows, cols)]):
             send(
                 precv.at[2, pl.ds(d * HALF + start, rows), cols],
-                far.at[d, pl.ds(start, rows), cols], far_sent, f_rs.at[0], (up, down)[d],
+                far.at[d, pl.ds(start, rows), cols], ring_sent, f_rs.at[0], (up, down)[d],
             )
     for r, odd in ((0, 3), (1, 1)):
         source = precv.at[2, pl.ds(CORNER_ROWS[r], CHUNK), tails[0]]
@@ -240,7 +240,7 @@
 
             @pl.when((y == odd) == (way != r))
             def _(r=r, way=way, source=source):
-                send(source, corner.at[way, r], corner_sent, f_rs.at[1], (up, down)[way])
+                send(source, corner.at[way, r], ring_sent, f_rs.at[1], (up, down)[way])
 
     signal_far(reply, False)
     for peer in (up, down):
@@ -272,7 +272,7 @@
         send(
             precv.at[((1, 3)[d], *window)],
             near.at[(d, *window)],
-            near_sent, n_rs.at[i], (up, down)[d],
+            ring_sent, n_rs.at[i], (up, down)[d],
         )
 
     def widen_early():
@@ -489,13 +489,11 @@
         approx[:, cols] = value
         new_error[:, cols] -= value
     wait(to_partner_sent, psend)
-    wait(far_sent, but_corners)
-    wait(corner_sent, corner.at[0])
     for i, (first, rows) in enumerate(LAST):
         wait(n_rs.at[1 + i], near.at[0, pl.ds(0, 2 * rows)])
         add_near(0, first, rows)
         add_near(1, HALF + first, rows)
-    wait(near_sent, near)
+    wait(ring_sent, psend.at[pl.ds(0, 3)])
 
 
 def reduce_buffers(width, quartered):
@@ -552,7 +550,7 @@
             reduce_buffers(ROWS, False),
             reduce_buffers(WIDE, True),
             dma((5,)),
-            dma((5,)),
+            dma((3,)),
             dma((8,)),
             dma((2,)),
             dma((4,)),

time: 76.1 us -> 76 us (level)
  no operation moved by 1% of the time
where the time goes in v7:
time: 76 us; the launch traced here: 75.9 us
  Pallas kernels  75.2 us (99%)
    pallas_call x1, Pallas kernels, body(): pl.pallas_call(main_kernel, out_shape=(pltpu.VMEM((OWN, COLS), F32), pltp...  73.1 us
    pallas_call x1, Pallas kernels, body(): pl.pallas_call(out_kernel, out_shape=(jax.ShapeDtypeStruct((OWN, COLS), F...  2.15 us

profile of v7, /device:TPU:1, one launch (start us, length us, event | category | flops | bytes accessed | tf_op | source)
XLA Modules:
  0.0 75.9 jit_solution(14718972880253410684)
XLA Ops:
  0.6 73.1 %shard_map.58 = (f32[128,3968]{1,0:T(8,128)S(1)}, f32[128,3968]{1,0:T(8,128)S(1)}, f32[32,3968]{1,0:T(8,128)S(1)}) custom-call(bf16[1,1,1024,3968]{3,2,1,0:T(8,128)(2,1)} %g_hbm.1, f32[1,128,3968]{2,1,0:T(8,128)} %e_hbm.1, f32[32,3968]{1,0:T(8,128)} %q_hbm.1), custom_call_target="tpu_custom_call" | custom-call | flops 2147483648 | bytes 14680064 | tf_op jit(solution)/shard_map/pallas_call | solution.py:528
  73.7 2.1 %shard_map.59 = (f32[128,3968]{1,0:T(8,128)}, f32[1,128,3968]{2,1,0:T(8,128)}, f32[32,3968]{1,0:T(8,128)}) custom-call(f32[128,3968]{1,0:T(8,128)S(1)} %get-tuple-element.6.approx, f32[128,3968]{1,0:T(8,128)S(1)} %get-tuple-element.7.new_error, f32[32,3968]{1,0:T(8,128)S(1)} %get-tuple-element.8.q_next), custom_call_target="tpu_custom_call" | custom-call | tf_op jit(solution)/shard_map/pallas_call | solution.py:571
